TPU v7x, 32 devices: a whole 2x2x4 slice. The times are simulated.
32 devices in a mesh: group: 4 (over y, x), chan: 8 (over z, core).
Axes of the slice: x: 2, y: 2, z: 4, core: 2. Of those that a mesh axis runs over, the one named last changes fastest.
Arguments:
- hidden_in: bfloat16 [8192, 768], P(('group', 'chan')), may hold values from -6 to 6
- mix_gain: float32 [768], replicated, may hold values from 0.5 to 1.5
- mix_shift: float32 [768], replicated, may hold values from -4 to 4
- w_query: bfloat16 [768, 768], P(None, 'chan'), may hold values from -0.21875 to 0.21875
- bias_query: float32 [768], P('chan'), may hold values from -4 to 4
- w_key: bfloat16 [768, 768], P(None, 'chan'), may hold values from -0.21875 to 0.21875
- bias_key: float32 [768], P('chan'), may hold values from -4 to 4
- w_value: bfloat16 [768, 768], P(None, 'chan'), may hold values from -0.21875 to 0.21875
- bias_value: float32 [768], P('chan'), may hold values from -4 to 4
- shift_taps: float32 [768, 4], P('chan'), may hold values from -3 to 3
- log_step: float32 [768], P('chan'), may hold values from -6.9 to -2.3
- log_decay: float32 [768, 32], P('chan'), may hold values from -1.6 to 0
- frequency: float32 [768, 32], P('chan'), may hold values from 0 to 30
- out_real: float32 [768, 32], P('chan'), may hold values from -6 to 6
- out_imag: float32 [768, 32], P('chan'), may hold values from -6 to 6
- skip_gain: float32 [768], P('chan'), may hold values from -6 to 6
- w_out: bfloat16 [768, 768], P('chan'), may hold values from -0.21875 to 0.21875
- bias_out: float32 [768], replicated, may hold values from -4 to 4
- mlp_gain: float32 [768], replicated, may hold values from 0.5 to 1.5
- mlp_shift: float32 [768], replicated, may hold values from -4 to 4
- w_up: bfloat16 [768, 3072], P(None, 'chan'), may hold values from -0.21875 to 0.21875
- bias_up: float32 [3072], P('chan'), may hold values from -4 to 4
- w_down: bfloat16 [3072, 768], P('chan'), may hold values from -0.109375 to 0.109375
- bias_down: float32 [768], replicated, may hold values from -4 to 4
- cotangent: bfloat16 [8192, 768], P(('group', 'chan')), may hold values from -6 to 6
- seq_blocks: int32 [4, 3], P('group'), may hold values from 0 to 16, as said below
Outputs:
- output: bfloat16 [8192, 768], P(('group', 'chan'))
- grad_input: bfloat16 [8192, 768], P(('group', 'chan'))
- grad_mix_gain: float32 [768], P('chan')
- grad_mix_shift: float32 [768], P('chan')
- grad_w_query: float32 [768, 768], P(None, 'chan')
- grad_bias_query: float32 [768], P('chan')
- grad_w_key: float32 [768, 768], P(None, 'chan')
- grad_bias_key: float32 [768], P('chan')
- grad_w_value: float32 [768, 768], P(None, 'chan')
- grad_bias_value: float32 [768], P('chan')
- grad_shift_taps: float32 [768, 4], P('chan')
- grad_log_step: float32 [768], P('chan')
- grad_log_decay: float32 [768, 32], P('chan')
- grad_frequency: float32 [768, 32], P('chan')
- grad_out_real: float32 [768, 32], P('chan')
- grad_out_imag: float32 [768, 32], P('chan')
- grad_skip_gain: float32 [768], P('chan')
- grad_w_out: float32 [768, 768], P('chan')
- grad_bias_out: float32 [768], P('chan')
- grad_mlp_gain: float32 [768], P('chan')
- grad_mlp_shift: float32 [768], P('chan')
- grad_w_up: float32 [768, 3072], P(None, 'chan')
- grad_bias_up: float32 [3072], P('chan')
- grad_w_down: float32 [3072, 768], P('chan')
- grad_bias_down: float32 [768], P('chan')
Inputs may be any that keep to these rules, and one draw needn't show every extreme that they name: `seq_blocks`: row g holds the lengths, in blocks of 128 rows and in order, of the three sequences that fill group g; they sum to 16, the first and the last are 0 or 1.
All inputs are finite; a program needn't handle non-finite values.
Results may differ from a plain program's by a relative error of at most 0.0087.
Values may be sent and summed in bfloat16 or wider, within the bound.
No kernel may reach another device: no remote copies, remote signals or barrier semaphores. Data moves between devices by JAX's collectives and lax.ppermute only.
A program may use at most 256 MiB of HBM per device.

v0:
```python
import jax
import jax.numpy as jnp
from jax import lax
from jax.sharding import PartitionSpec as P

STRETCH = 128


epsilon = 1e-05
exact_precision = lax.Precision.HIGHEST


def layer_norm(values, gain, shift):
    center = values - jnp.mean(values, axis=-1, keepdims=True)
    spread = jnp.mean(center * center, axis=-1, keepdims=True)
    return center * lax.rsqrt(spread + epsilon) * gain + shift


def gelu_tanh(values):
    return jax.nn.gelu(values, approximate=True)


def ssm_tables(log_step, log_decay, frequency, out_real, out_imag):
    step_size = jnp.exp(log_step)[:, None]
    rate = -jnp.exp(log_decay)
    decay = rate * step_size
    turn = frequency * step_size
    growth = jnp.exp(decay)
    ratio_re = growth * jnp.cos(turn) - 1.0
    ratio_im = growth * jnp.sin(turn)
    denom = rate * rate + frequency * frequency
    scaled_re = (ratio_re * rate + ratio_im * frequency) / denom
    scaled_im = (ratio_im * rate - ratio_re * frequency) / denom
    weight_re = out_real * scaled_re - out_imag * scaled_im
    weight_im = out_real * scaled_im + out_imag * scaled_re
    return (decay, turn, weight_re, weight_im)


def combine_states(earlier, later):
    early_cr, early_ci, early_er, early_ei = earlier
    late_cr, late_ci, late_er, late_ei = later
    return (
        late_cr * early_cr - late_ci * early_ci,
        late_cr * early_ci + late_ci * early_cr,
        late_cr * early_er - late_ci * early_ei + late_er,
        late_cr * early_ei + late_ci * early_er + late_ei,
    )


def mixer_core(
    query,
    key_rows,
    value_rows,
    shift_taps,
    log_step,
    log_decay,
    frequency,
    out_real,
    out_imag,
    skip_gain,
    bounds,
):
    first, second = bounds
    query_cols = query.T
    key_cols = key_rows.T
    value_cols = value_rows.T
    channels, total = query_cols.shape
    width = STRETCH
    count = total // width
    rows = jnp.arange(total, dtype=jnp.int32)
    block_of = rows // width
    start_block = jnp.where(block_of >= second, second, jnp.where(block_of >= first, first, 0))
    place = rows - start_block * width
    shifted = key_cols * shift_taps[:, 0:1]
    for offset in range(1, shift_taps.shape[1]):
        moved = jnp.pad(key_cols[:, :-offset], ((0, 0), (offset, 0)))
        shifted = (
            shifted
            + jnp.where((place >= offset)[None, :], moved, 0.0) * shift_taps[:, offset : offset + 1]
        )
    product = shifted * value_cols
    blocks = product.reshape(channels, count, width)
    decay, turn, weight_re, weight_im = ssm_tables(
        log_step, log_decay, frequency, out_real, out_imag
    )
    times = jnp.arange(width + 1, dtype=jnp.float32)
    magnitude = jnp.exp(decay[:, :, None] * times)
    power_re = magnitude * jnp.cos(turn[:, :, None] * times)
    power_im = magnitude * jnp.sin(turn[:, :, None] * times)
    kernel = 2.0 * jnp.sum(
        weight_re[:, :, None] * power_re[:, :, :width]
        - weight_im[:, :, None] * power_im[:, :, :width],
        axis=1,
    )
    lags = jnp.arange(width, dtype=jnp.int32)[:, None] - jnp.arange(width, dtype=jnp.int32)[None, :]
    toeplitz = jnp.where(lags >= 0, kernel[:, jnp.maximum(lags, 0)], 0.0)
    within_block = jnp.einsum("cij,ckj->cki", toeplitz, blocks, precision=exact_precision)
    reverse_re = power_re[:, :, :width][:, :, ::-1]
    reverse_im = power_im[:, :, :width][:, :, ::-1]
    ending_re = jnp.einsum("cms,cks->ckm", reverse_re, blocks, precision=exact_precision)
    ending_im = jnp.einsum("cms,cks->ckm", reverse_im, blocks, precision=exact_precision)
    block_ids = jnp.arange(count, dtype=jnp.int32)
    begins = jnp.logical_or(block_ids == first, block_ids == second)
    keep = jnp.where(begins, 0.0, 1.0).astype(jnp.float32)[None, :, None]
    mult_re = power_re[:, None, :, width] * keep
    mult_im = power_im[:, None, :, width] * keep
    unused_re, unused_im, after_re, after_im = lax.associative_scan(
        combine_states, (mult_re, mult_im, ending_re, ending_im), axis=1
    )
    state_re = jnp.pad(after_re[:, :-1], ((0, 0), (1, 0), (0, 0))) * keep
    state_im = jnp.pad(after_im[:, :-1], ((0, 0), (1, 0), (0, 0))) * keep
    table_re = (
        weight_re[:, :, None] * power_re[:, :, 1:] - weight_im[:, :, None] * power_im[:, :, 1:]
    )
    table_im = (
        weight_re[:, :, None] * power_im[:, :, 1:] + weight_im[:, :, None] * power_re[:, :, 1:]
    )
    carried = 2.0 * (
        jnp.einsum("cmt,ckm->ckt", table_re, state_re, precision=exact_precision)
        - jnp.einsum("cmt,ckm->ckt", table_im, state_im, precision=exact_precision)
    )
    conv = (within_block + carried).reshape(channels, total) + skip_gain[:, None] * product
    return (query_cols * conv).T


def channel_plan(
    hidden_in,
    mix_gain,
    mix_shift,
    w_query,
    bias_query,
    w_key,
    bias_key,
    w_value,
    bias_value,
    shift_taps,
    log_step,
    log_decay,
    frequency,
    out_real,
    out_imag,
    skip_gain,
    w_out,
    bias_out,
    mlp_gain,
    mlp_shift,
    w_up,
    bias_up,
    w_down,
    bias_down,
    cotangent,
    bounds,
):
    channels = w_query.shape[1]
    inputs = hidden_in.astype(jnp.float32)
    normed, first_back = jax.vjp(layer_norm, inputs, mix_gain, mix_shift)
    normed_low = normed.astype(jnp.bfloat16)
    w_proj = jnp.concatenate([w_query, w_key, w_value], axis=1)
    bias_proj = jnp.concatenate([bias_query, bias_key, bias_value])
    gathered = lax.all_gather(normed_low, "chan", axis=0, tiled=True)
    projected = jnp.dot(gathered, w_proj, preferred_element_type=jnp.float32)
    projected = projected + bias_proj
    query = projected[:, :channels]
    key_rows = projected[:, channels : 2 * channels]
    value_rows = projected[:, 2 * channels :]

    def core_of(
        query_in, key_in, value_in, taps, step_log, decay_log, freq, real_part, imag_part, direct
    ):
        return mixer_core(
            query_in,
            key_in,
            value_in,
            taps,
            step_log,
            decay_log,
            freq,
            real_part,
            imag_part,
            direct,
            bounds,
        )

    core, core_back = jax.vjp(
        core_of,
        query,
        key_rows,
        value_rows,
        shift_taps,
        log_step,
        log_decay,
        frequency,
        out_real,
        out_imag,
        skip_gain,
    )
    core_low = core.astype(jnp.bfloat16)
    mixer = lax.psum_scatter(
        jnp.dot(core_low, w_out, preferred_element_type=jnp.float32),
        "chan",
        scatter_dimension=0,
        tiled=True,
    )
    residual = inputs + mixer + bias_out
    normed_two, second_back = jax.vjp(layer_norm, residual, mlp_gain, mlp_shift)
    normed_two_low = normed_two.astype(jnp.bfloat16)
    gathered_two = lax.all_gather(normed_two_low, "chan", axis=0, tiled=True)
    upward = jnp.dot(gathered_two, w_up, preferred_element_type=jnp.float32)
    upward = upward + bias_up
    active, active_back = jax.vjp(gelu_tanh, upward)
    active_low = active.astype(jnp.bfloat16)
    branch = lax.psum_scatter(
        jnp.dot(active_low, w_down, preferred_element_type=jnp.float32),
        "chan",
        scatter_dimension=0,
        tiled=True,
    )
    output = (residual + branch + bias_down).astype(jnp.bfloat16)
    outgoing = cotangent.astype(jnp.float32)
    grad_bias_down = jnp.sum(outgoing, axis=0)
    piece = lax.all_gather(cotangent, "chan", axis=0, tiled=True)
    grad_down = jnp.einsum("tf,td->fd", active_low, piece, preferred_element_type=jnp.float32)
    rows_back = jnp.einsum("td,fd->tf", piece, w_down, preferred_element_type=jnp.float32)
    grad_active = rows_back
    (grad_upward,) = active_back(grad_active)
    grad_up_low = grad_upward.astype(jnp.bfloat16)
    grad_bias_up = jnp.sum(grad_up_low, axis=0, dtype=jnp.float32)
    grad_normed_two = lax.psum_scatter(
        jnp.einsum("tf,df->td", grad_up_low, w_up, preferred_element_type=jnp.float32),
        "chan",
        scatter_dimension=0,
        tiled=True,
    )
    grad_w_up = jnp.einsum(
        "td,tf->df", gathered_two, grad_up_low, preferred_element_type=jnp.float32
    )
    grad_res_two, grad_mlp_gain, grad_mlp_shift = second_back(grad_normed_two)
    grad_residual = outgoing + grad_res_two
    grad_bias_out = jnp.sum(grad_residual, axis=0)
    grad_res_low = grad_residual.astype(jnp.bfloat16)
    piece = lax.all_gather(grad_res_low, "chan", axis=0, tiled=True)
    grad_outw = jnp.einsum("tc,td->cd", core_low, piece, preferred_element_type=jnp.float32)
    rows_back = jnp.einsum("td,cd->tc", piece, w_out, preferred_element_type=jnp.float32)
    (
        grad_query,
        grad_key,
        grad_value,
        grad_shift_taps,
        grad_log_step,
        grad_log_decay,
        grad_frequency,
        grad_out_real,
        grad_out_imag,
        grad_skip_gain,
    ) = core_back(rows_back)
    grad_proj_low = jnp.concatenate([grad_query, grad_key, grad_value], axis=1).astype(jnp.bfloat16)
    grad_bias_proj = jnp.sum(grad_proj_low, axis=0, dtype=jnp.float32)
    grad_normed = lax.psum_scatter(
        jnp.einsum("tc,dc->td", grad_proj_low, w_proj, preferred_element_type=jnp.float32),
        "chan",
        scatter_dimension=0,
        tiled=True,
    )
    grad_w_proj = jnp.einsum(
        "td,tc->dc", gathered, grad_proj_low, preferred_element_type=jnp.float32
    )
    grad_in_norm, grad_mix_gain, grad_mix_shift = first_back(grad_normed)
    grad_input = (grad_residual + grad_in_norm).astype(jnp.bfloat16)
    (
        share_mix_gain,
        share_mix_shift,
        share_bias_out,
        share_mlp_gain,
        share_mlp_shift,
        share_bias_down,
    ) = (
        lax.psum_scatter(grad_mix_gain, "chan", scatter_dimension=0, tiled=True),
        lax.psum_scatter(grad_mix_shift, "chan", scatter_dimension=0, tiled=True),
        lax.psum_scatter(grad_bias_out, "chan", scatter_dimension=0, tiled=True),
        lax.psum_scatter(grad_mlp_gain, "chan", scatter_dimension=0, tiled=True),
        lax.psum_scatter(grad_mlp_shift, "chan", scatter_dimension=0, tiled=True),
        lax.psum_scatter(grad_bias_down, "chan", scatter_dimension=0, tiled=True),
    )
    return (
        output,
        grad_input,
        grad_w_proj,
        grad_bias_proj,
        grad_shift_taps,
        grad_log_step,
        grad_log_decay,
        grad_frequency,
        grad_out_real,
        grad_out_imag,
        grad_skip_gain,
        grad_outw,
        grad_w_up,
        grad_bias_up,
        grad_down,
        share_mix_gain,
        share_mix_shift,
        share_bias_out,
        share_mlp_gain,
        share_mlp_shift,
        share_bias_down,
    )


def local(
    hidden_in,
    mix_gain,
    mix_shift,
    w_query,
    bias_query,
    w_key,
    bias_key,
    w_value,
    bias_value,
    shift_taps,
    log_step,
    log_decay,
    frequency,
    out_real,
    out_imag,
    skip_gain,
    w_out,
    bias_out,
    mlp_gain,
    mlp_shift,
    w_up,
    bias_up,
    w_down,
    bias_down,
    cotangent,
    seq_blocks,
):
    channels = w_query.shape[1]
    first_start = seq_blocks[0, 0]
    second_start = seq_blocks[0, 0] + seq_blocks[0, 1]
    bounds = (first_start, second_start)
    arguments = (
        hidden_in,
        mix_gain,
        mix_shift,
        w_query,
        bias_query,
        w_key,
        bias_key,
        w_value,
        bias_value,
        shift_taps,
        log_step,
        log_decay,
        frequency,
        out_real,
        out_imag,
        skip_gain,
        w_out,
        bias_out,
        mlp_gain,
        mlp_shift,
        w_up,
        bias_up,
        w_down,
        bias_down,
        cotangent,
        bounds,
    )
    results = channel_plan(*arguments)
    (
        output,
        grad_input,
        grad_w_proj,
        grad_bias_proj,
        grad_shift_taps,
        grad_log_step,
        grad_log_decay,
        grad_frequency,
        grad_out_real,
        grad_out_imag,
        grad_skip_gain,
        grad_w_out,
        grad_w_up,
        grad_bias_up,
        grad_w_down,
        share_mix_gain,
        share_mix_shift,
        share_bias_out,
        share_mlp_gain,
        share_mlp_shift,
        share_bias_down,
    ) = results
    (
        sum_w_proj,
        sum_bias_proj,
        sum_shift_taps,
        sum_log_step,
        sum_log_decay,
        sum_frequency,
        sum_out_real,
        sum_out_imag,
        sum_skip_gain,
        sum_w_out,
        sum_w_up,
        sum_bias_up,
        sum_w_down,
        sum_mix_gain,
        sum_mix_shift,
        sum_bias_out,
        sum_mlp_gain,
        sum_mlp_shift,
        sum_bias_down,
    ) = lax.psum(
        (
            grad_w_proj,
            grad_bias_proj,
            grad_shift_taps,
            grad_log_step,
            grad_log_decay,
            grad_frequency,
            grad_out_real,
            grad_out_imag,
            grad_skip_gain,
            grad_w_out,
            grad_w_up,
            grad_bias_up,
            grad_w_down,
            share_mix_gain,
            share_mix_shift,
            share_bias_out,
            share_mlp_gain,
            share_mlp_shift,
            share_bias_down,
        ),
        "group",
    )
    return (
        output,
        grad_input,
        sum_mix_gain,
        sum_mix_shift,
        sum_w_proj[:, :channels],
        sum_bias_proj[:channels],
        sum_w_proj[:, channels : 2 * channels],
        sum_bias_proj[channels : 2 * channels],
        sum_w_proj[:, 2 * channels :],
        sum_bias_proj[2 * channels :],
        sum_shift_taps,
        sum_log_step,
        sum_log_decay,
        sum_frequency,
        sum_out_real,
        sum_out_imag,
        sum_skip_gain,
        sum_w_out,
        sum_bias_out,
        sum_mlp_gain,
        sum_mlp_shift,
        sum_w_up,
        sum_bias_up,
        sum_w_down,
        sum_bias_down,
    )


def solution(mesh):
    return jax.shard_map(
        local,
        mesh=mesh,
        in_specs=(
            P(("group", "chan"), None),
            P(),
            P(),
            P(None, "chan"),
            P("chan"),
            P(None, "chan"),
            P("chan"),
            P(None, "chan"),
            P("chan"),
            P("chan", None),
            P("chan"),
            P("chan", None),
            P("chan", None),
            P("chan", None),
            P("chan", None),
            P("chan"),
            P("chan", None),
            P(),
            P(),
            P(),
            P(None, "chan"),
            P("chan"),
            P("chan", None),
            P(),
            P(("group", "chan"), None),
            P("group", None),
        ),
        out_specs=(
            P(("group", "chan"), None),
            P(("group", "chan"), None),
            P("chan"),
            P("chan"),
            P(None, "chan"),
            P("chan"),
            P(None, "chan"),
            P("chan"),
            P(None, "chan"),
            P("chan"),
            P("chan", None),
            P("chan"),
            P("chan", None),
            P("chan", None),
            P("chan", None),
            P("chan", None),
            P("chan"),
            P("chan", None),
            P("chan"),
            P("chan"),
            P("chan"),
            P(None, "chan"),
            P("chan"),
            P("chan", None),
            P("chan"),
        ),
        check_vma=False,
    )
```

profile of v0, /device:TPU:0, one launch (start us, length us, event | category | flops | bytes accessed | tf_op | source)
XLA Modules:
  0.0 1010.6 jit_solution(13684451682947008110)
XLA Ops:
  16.5 13.2 %fusion.18 = (f32[96,32,129]{2,1,0:T(8,128)S(1)}, f32[96,32,129]{2,1,0:T(8,128)}) fusion(f32[96,32]{1,0:T(8,128)S(1)} %copy.177, f32[96,32]{1,0:T(8,128)S(1)} %copy.176), kind=kLoop, calls=%fused_computation.31 | loop fusion | flops 1585152 | bytes 3194880 | tf_op jit(solution)/shard_map/jvp()/mul | solution.py:89
  35.0 3.3 subtract_reduce_fusion
  38.4 3.7 rev.12
  44.2 54.5 %gather_fusion = f32[16384,96]{1,0:T(8,128)} fusion(f32[96,128]{0,1:T(8,128)S(1)} %copy.179, s32[16384]{0:T(1024)S(1)} %broadcast_clamp_fusion), kind=kCustom, calls=%fused_computation | custom fusion | bytes 12648448 | tf_op jit(solution)/shard_map/jvp()/gather | solution.py:96
  98.7 8.7 copy.180
  112.4 3.2 convolution_add_fusion.1
  122.2 3.1 slice.338
  128.5 3.2 slice.383
  131.7 3.9 fusion.138
  143.4 3.2 slice.388
  183.9 3.3 pad.393
  188.6 3.3 pad.391
  192.0 3.3 pad.392
  195.3 3.3 pad.394
  212.7 4.8 pad.749
  226.7 6.0 fusion.63
  232.7 4.6 fusion.27
  237.4 11.9 %fusion.21 = f32[96,16,128]{2,1,0:T(8,128)S(1)} fusion(f32[96,16,128]{2,1,0:T(8,128)S(1)} %fusion.27, f32[96,16,128]{2,1,0:T(8,128)S(1)} %bitcast.143, f32[128,128,96]{1,0,2:T(8,128)} %copy.180, pred[128,128]{1,0:T(8,128)(4,1)S(1)} %copy-done.83), kind=kOutput, calls=%fused_computation.49 | convolution fusion | flops 303759360 | bytes 8667136 | tf_op jit(solution)/shard_map/jvp(cij,ckj->cki)/dot_general | solution.py:97
  251.9 3.6 fusion.139
  256.3 71.9 %reduce-scatter.5.cloned.1.call-done = f32[256,768]{1,0:T(8,128)} async-done(((f32[2048,768]{1,0:T(8,128)}), f32[256,768]{1,0:T(8,128)}) %reduce-scatter.5.cloned.1.call-update) | async-done | bytes 786448 | tf_op jit(solution)/shard_map/reduce_scatter | solution.py:198
  330.8 9.9 reduce-scatter.9.cloned.1.call-start
  340.7 25.8 %all-gather.9.cloned.1.call-done = bf16[2048,768]{1,0:T(8,128)(2,1)} async-done(((bf16[256,768]{1,0:T(8,128)(2,1)}), bf16[2048,768]{1,0:T(8,128)(2,1)}) %all-gather.9.cloned.1.call-update) | async-done | bytes 3145744 | tf_op jit(solution)/shard_map/all_gather | solution.py:221
  366.5 5.5 fusion.140
  372.0 33.8 %all-gather.7.cloned.1.call-done = bf16[2048,768]{1,0:T(8,128)(2,1)} async-done(((bf16[256,768]{1,0:T(8,128)(2,1)}), bf16[2048,768]{1,0:T(8,128)(2,1)}) %all-gather.7.cloned.1.call-update) | async-done | bytes 3145744 | tf_op jit(solution)/shard_map/all_gather | solution.py:207
  405.8 8.8 convert_reduce_fusion
  415.8 4.5 fusion.141
  421.3 6.8 fusion.112
  428.2 60.9 %reduce-scatter.9.cloned.1.call-done = f32[256,768]{1,0:T(8,128)} async-done(((f32[2048,768]{1,0:T(8,128)}), f32[256,768]{1,0:T(8,128)}) %reduce-scatter.9.cloned.1.call-update) | async-done | bytes 786448 | tf_op jit(solution)/shard_map/reduce_scatter | solution.py:228
  491.2 68.3 %reduce-scatter.7.cloned.1.call-done = f32[256,768]{1,0:T(8,128)} async-done(((f32[2048,768]{1,0:T(8,128)}), f32[256,768]{1,0:T(8,128)}) %reduce-scatter.7.cloned.1.call-update) | async-done | bytes 786448 | tf_op jit(solution)/shard_map/reduce_scatter | solution.py:212
  565.9 5.2 fusion.146
  571.1 4.6 fusion.111
  575.7 24.9 %all-gather.11.cloned.1.call-done = bf16[2048,768]{1,0:T(8,128)(2,1)} async-done(((bf16[256,768]{1,0:T(8,128)(2,1)}), bf16[2048,768]{1,0:T(8,128)(2,1)}) %all-gather.11.cloned.1.call-update) | async-done | bytes 3145744 | tf_op jit(solution)/shard_map/all_gather | solution.py:241
  600.6 5.0 multiply_reduce_fusion.10
  606.6 4.6 fusion.53
  611.2 5.0 fusion.48
  650.5 3.3 pad.437
  655.6 3.3 pad.442
  658.9 3.3 pad.475
  664.9 3.3 pad.478
  668.2 3.3 pad.476
  671.5 3.3 pad.479
  674.8 3.3 pad.447
  688.7 4.8 pad.451
  693.5 4.8 pad.443
  703.4 4.8 pad.452
  708.2 4.7 pad.403
  712.8 4.6 pad.450
  725.4 3.3 fusion.142
  730.4 7.7 fusion.24
  746.0 5.9 fusion.109
  757.5 4.8 pad.488
  765.5 4.7 pad.487
  771.6 5.2 fusion.144
  776.8 3.6 rev.15
  780.4 3.9 fusion.143
  784.4 3.7 rev.14
  791.7 11.8 %select_bitcast_fusion = f32[128,128,96]{1,0,2:T(8,128)} fusion(pred[128,128]{1,0:T(8,128)(4,1)S(1)} %copy-done.84, f32[96,16,128]{2,1,0:T(8,128)S(1)} %bitcast.132, f32[96,16,128]{2,1,0:T(8,128)S(1)} %bitcast.146), kind=kOutput, calls=%fused_computation.6 | convolution fusion | flops 303562752 | bytes 7880704 | tf_op jit(solution)/shard_map/transpose(jvp(cij,ckj->cki))/dot_general | solution.py:97
  803.5 8.6 copy.220
  812.1 98.6 %scatter_custom_fusion = f32[96,128]{0,1:T(8,128)S(1)} fusion(s32[16384]{0:T(1024)} %maximum_bitcast_fusion, f32[16384,96]{1,0:T(8,128)} %bitcast.152, f32[]{:T(128)} %constant.67.clone.1), kind=kCustom, calls=%fused_computation.228 | custom fusion | flops 1572864 | bytes 49664 | tf_op jit(solution)/shard_map/transpose(jvp())/scatter-add | solution.py:96
  910.7 3.9 fusion.51
  914.7 10.6 %multiply_reduce_fusion.8 = (f32[96,32]{1,0:T(8,128)}, f32[96,32]{1,0:T(8,128)}, f32[96,32]{1,0:T(8,128)}, f32[96,32]{1,0:T(8,128)}, f32[96,32]{1,0:T(8,128)}, /...) fusion(f32[96,32,129]{2,1,0:T(8,128)} %get-tuple-element.245, ...), kind=kOutput, calls=%fused_computation.44 | convolution fusion | flops 83343360 | bytes 18481152 | tf_op jit(solution)/shard_map/transpose(jvp(cmt,ckm->ckt))/dot_general | solution.py:120
  925.6 18.4 %multiply_reduce_fusion = (f32[96,32]{1,0:T(8,128)S(1)}, f32[96,32]{1,0:T(8,128)S(1)}, f32[96,32]{1,0:T(8,128)S(1)}) fusion(f32[96,32]{1,0:T(8,128)S(1)} %copy-done.75, f32[96,32]{1,0:T(8,128)S(1)} %copy-done.77, f32[96,32,128]{2,1,0:T(8,128)S(1)} %get-tuple-element.238, f32[96,32,128]{2,1,0:T(8,128)S(1)} %copy-done.26, f32[96,32,1]{2,1,0:T(8,128)S(1)} %copy-done.27, ...), kind=kLoop, calls=%fused_computation.21 | loop fusion | flops 9897984 | bytes 12668928 | tf_op jit(solution)/shard_map/transpose(jvp())/reduce_sum | solution.py:87
  952.9 26.4 %all-reduce.100 = (f32[768]{0:T(1024)S(1)}, f32[768]{0:T(1024)S(1)}, f32[768]{0:T(1024)S(1)}, f32[768]{0:T(1024)S(1)}, f32[768]{0:T(1024)S(1)}, /*index=5*/f32[768]{0:T(1024)S(1)}) all-reduce(f32[768]{0:T(1024)S(1)} %get-tuple-element.88, f32[768]{0:T(1024)S(1)} %get-tuple-element.95, ...), channel_id=6, replica_groups=mesh['group'=4,'chan'=8] {'chan'}, use_global_device_ids=true, to_apply=%region_14.15.clone | all-reduce | flops 4608 | bytes 36864
  979.7 18.0 %all-reduce.101 = (f32[96]{0:T(128)}, f32[96]{0:T(128)}, f32[288]{0:T(512)S(1)}, f32[96,4]{0,1:T(4,128)}, f32[96]{0:T(128)}, /*index=5*/f32[96,32]{0,1:T(8,128)}...) all-reduce(f32[96]{0:T(128)S(1)} %dynamic-slice.1, ...), channel_id=1, replica_groups=mesh['group'=4,'chan'=8] {'group'}, use_global_device_ids=true, to_apply=%region_15.16 | all-reduce | flops 14112 | bytes 112896 | tf_op jit(solution)/shard_map/psum | solution.py:413
  (578 shorter events, 216.6 us)
Async XLA Ops:
  7.2 398.6 %copy-start = (bf16[768,384]{1,0:T(8,128)(2,1)S(1)}, bf16[768,384]{1,0:T(8,128)(2,1)}, u32[]{:S(2)}) copy-start(bf16[768,384]{1,0:T(8,128)(2,1)} %param.46) | copy-start | bytes 1769476
  7.2 105.2 %all-gather.5.cloned.1.call-start = ((), (), s32[]{:S(2)}) async-start(), calls=%async_computation.4 | async-start | bytes 3538944 | tf_op jit(solution)/shard_map/all_gather | solution.py:160
  12.9 315.3 %reduce-scatter.5.cloned.1.call-start = ((), (), s32[]{:S(2)}) async-start(), calls=%async_computation.5 | async-start | bytes 7077888 | tf_op jit(solution)/shard_map/reduce_scatter | solution.py:198
  14.4 15.3 %copy-start.86 = (f32[96,32]{0,1:T(8,128)}, f32[96,32]{0,1:T(8,128)S(1)}, u32[]{:S(2)}) copy-start(f32[96,32]{0,1:T(8,128)S(1)} %get-tuple-element.162) | copy-start | bytes 36868
  14.5 15.2 %copy-start.88 = (f32[96,32]{0,1:T(8,128)}, f32[96,32]{0,1:T(8,128)S(1)}, u32[]{:S(2)}) copy-start(f32[96,32]{0,1:T(8,128)S(1)} %sin.8) | copy-start | bytes 36868
  14.6 15.1 %copy-start.74 = (f32[96,32]{1,0:T(8,128)}, f32[96,32]{1,0:T(8,128)S(1)}, u32[]{:S(2)}) copy-start(f32[96,32]{1,0:T(8,128)S(1)} %copy.177) | copy-start | bytes 36868
  16.3 18.7 %copy-start.49 = (f32[96,32]{1,0:T(8,128)}, f32[96,32]{1,0:T(8,128)S(1)}, u32[]{:S(2)}) copy-start(f32[96,32]{1,0:T(8,128)S(1)} %copy.175) | copy-start | bytes 36868
  112.4 91.3 %copy-start.29 = (f32[96,16,32]{0,2,1:T(8,128)}, f32[96,16,32]{0,2,1:T(8,128)S(1)}, u32[]{:S(2)}) copy-start(f32[96,16,32]{0,2,1:T(8,128)S(1)} %get-tuple-element.286) | copy-start | bytes 589828
  112.4 91.3 %copy-start.31 = (f32[96,16,32]{0,2,1:T(8,128)}, f32[96,16,32]{0,2,1:T(8,128)S(1)}, u32[]{:S(2)}) copy-start(f32[96,16,32]{0,2,1:T(8,128)S(1)} %get-tuple-element.287) | copy-start | bytes 589828
  117.5 131.8 %copy-start.8 = (f32[96,2048]{1,0:T(8,128)}, f32[96,2048]{1,0:T(8,128)S(1)}, u32[]{:S(2)}) copy-start(f32[96,2048]{1,0:T(8,128)S(1)} %get-tuple-element.173) | copy-start | bytes 2359300
  204.8 17.7 %copy-start.145 = (f32[16]{0:T(128)S(1)}, f32[16]{0:T(128)}, u32[]{:S(2)}) copy-start(f32[16]{0:T(128)} %copy-done.144) | copy-start | bytes 196
  205.5 21.2 %copy-start.50 = (f32[96,32]{1,0:T(8,128)S(1)}, f32[96,32]{1,0:T(8,128)}, u32[]{:S(2)}) copy-start(f32[96,32]{1,0:T(8,128)} %copy-done.49) | copy-start | bytes 36868
  237.4 14.5 %copy-start.67 = (bf16[96,768]{1,0:T(8,128)(2,1)S(1)}, bf16[96,768]{1,0:T(8,128)(2,1)}, u32[]{:S(2)}) copy-start(bf16[96,768]{1,0:T(8,128)(2,1)} %param.42) | copy-start | bytes 442372
  255.5 72.7 %copy-start.7 = (bf16[256,768]{1,0:T(8,128)(2,1)S(1)}, bf16[256,768]{1,0:T(8,128)(2,1)}, u32[]{:S(2)}) copy-start(bf16[256,768]{1,0:T(8,128)(2,1)} %param.26) | copy-start | bytes 1179652
  255.5 72.7 %copy-start.155 = (f32[768]{0:T(1024)S(1)}, f32[768]{0:T(1024)}, u32[]{:S(2)}) copy-start(f32[768]{0:T(1024)} %param.43) | copy-start | bytes 9220
  255.5 74.2 %copy-start.119 = (f32[768]{0:T(1024)S(1)}, f32[768]{0:T(1024)}, u32[]{:S(2)}) copy-start(f32[768]{0:T(1024)} %param.44) | copy-start | bytes 9220
  255.5 74.2 %copy-start.156 = (f32[768]{0:T(1024)S(1)}, f32[768]{0:T(1024)}, u32[]{:S(2)}) copy-start(f32[768]{0:T(1024)} %param.45) | copy-start | bytes 9220
  255.6 111.0 %all-gather.9.cloned.1.call-start = ((), (), s32[]{:S(2)}) async-start(), calls=%async_computation.8 | async-start | bytes 3538944 | tf_op jit(solution)/shard_map/all_gather | solution.py:221
  256.3 149.5 %all-gather.7.cloned.1.call-start = ((), (), s32[]{:S(2)}) async-start(), calls=%async_computation.6 | async-start | bytes 3538944 | tf_op jit(solution)/shard_map/all_gather | solution.py:207
  330.8 75.0 %copy-start.170 = (f32[384]{0:T(512)S(1)}, f32[384]{0:T(512)}, u32[]{:S(2)}) copy-start(f32[384]{0:T(512)} %param.47) | copy-start | bytes 4612
  330.8 158.3 %reduce-scatter.9.cloned.1.call-start = ((), (), s32[]{:S(2)}) async-start(), calls=%async_computation.9 | async-start | bytes 7077888 | tf_op jit(solution)/shard_map/reduce_scatter | solution.py:228
  420.3 139.2 %reduce-scatter.7.cloned.1.call-start = ((), (), s32[]{:S(2)}) async-start(), calls=%async_computation.7 | async-start | bytes 7077888 | tf_op jit(solution)/shard_map/reduce_scatter | solution.py:212
  428.1 131.4 %copy-start.157 = (f32[768]{0:T(1024)S(1)}, f32[768]{0:T(1024)}, u32[]{:S(2)}) copy-start(f32[768]{0:T(1024)} %param.49) | copy-start | bytes 9220
  428.1 134.7 %copy-start.43 = (bf16[256,768]{1,0:T(8,128)(2,1)S(1)}, bf16[256,768]{1,0:T(8,128)(2,1)}, u32[]{:S(2)}) copy-start(bf16[256,768]{1,0:T(8,128)(2,1)} %param.50) | copy-start | bytes 1179652
  428.2 172.4 %all-gather.11.cloned.1.call-start = ((), (), s32[]{:S(2)}) async-start(), calls=%async_computation.10 | async-start | bytes 3538944 | tf_op jit(solution)/shard_map/all_gather | solution.py:241
  491.2 72.7 %copy-start.121 = (pred[2048]{0:T(1024)(128)(4,1)S(1)}, pred[2048]{0:T(1024)(128)(4,1)}, u32[]{:S(2)}) copy-start(pred[2048]{0:T(1024)(128)(4,1)} %copy-done.120) | copy-start | bytes 6148
  491.2 73.4 %copy-start.124 = (pred[2048]{0:T(1024)(128)(4,1)S(1)}, pred[2048]{0:T(1024)(128)(4,1)}, u32[]{:S(2)}) copy-start(pred[2048]{0:T(1024)(128)(4,1)} %copy-done.123) | copy-start | bytes 6148
  491.2 74.0 %copy-start.127 = (pred[2048]{0:T(1024)(128)(4,1)S(1)}, pred[2048]{0:T(1024)(128)(4,1)}, u32[]{:S(2)}) copy-start(pred[2048]{0:T(1024)(128)(4,1)} %copy-done.126) | copy-start | bytes 6148
  563.7 381.5 %all-reduce.105.cloned.1.call-start = ((), (), s32[]{:S(2)}) async-start(), calls=%async_computation.12 | async-start | bytes 7077888 | tf_op jit(solution)/shard_map/psum | solution.py:413
  571.0 29.5 %copy-start.9 = (f32[96,2048]{1,0:T(8,128)S(1)}, f32[96,2048]{1,0:T(8,128)}, u32[]{:S(2)}) copy-start(f32[96,2048]{1,0:T(8,128)} %copy-done.8) | copy-start | bytes 2359300
  571.0 29.5 %copy-start.68 = (bf16[96,768]{1,0:T(8,128)(2,1)S(1)}, bf16[96,768]{1,0:T(8,128)(2,1)}, u32[]{:S(2)}) copy-start(bf16[96,768]{1,0:T(8,128)(2,1)} %param.42) | copy-start | bytes 442372
  634.9 51.3 %slice-start.2 = ((f32[96,4,32]{0,2,1:T(8,128)}), f32[96,1,32]{0,2,1:T(8,128)S(1)}, s32[]{:S(2)}) async-start(f32[96,4,32]{0,2,1:T(8,128)} %copy-done.90), calls=%async_computation.15 | async-start | bytes 32768 | tf_op jit(solution)/shard_map/transpose(jvp())/split | solution.py:107
  634.9 51.3 %slice-start.3 = ((f32[96,4,32]{0,2,1:T(8,128)}), f32[96,1,32]{0,2,1:T(8,128)S(1)}, s32[]{:S(2)}) async-start(f32[96,4,32]{0,2,1:T(8,128)} %copy-done.91), calls=%async_computation.16 | async-start | bytes 32768 | tf_op jit(solution)/shard_map/transpose(jvp())/split | solution.py:107
  655.6 42.7 %copy-start.52 = (f32[96,8,32]{0,2,1:T(8,128)S(1)}, f32[96,8,32]{0,2,1:T(8,128)}, u32[]{:S(2)}) copy-start(f32[96,8,32]{0,2,1:T(8,128)} %copy.226) | copy-start | bytes 294916
  686.2 31.3 %slice-start.1 = ((f32[96,8,32]{0,2,1:T(8,128)}), f32[96,1,32]{0,2,1:T(8,128)S(1)}, s32[]{:S(2)}) async-start(f32[96,8,32]{0,2,1:T(8,128)} %copy-done.71), calls=%async_computation.14 | async-start | bytes 32768 | tf_op jit(solution)/shard_map/transpose(jvp())/split | solution.py:107
  688.7 32.8 %slice-start = ((f32[96,8,32]{0,2,1:T(8,128)}), f32[96,1,32]{0,2,1:T(8,128)S(1)}, s32[]{:S(2)}) async-start(f32[96,8,32]{0,2,1:T(8,128)} %copy-done.70), calls=%async_computation.13 | async-start | bytes 32768 | tf_op jit(solution)/shard_map/transpose(jvp())/split | solution.py:107
  700.4 21.1 %copy-start.59 = (f32[96,16,32]{0,2,1:T(8,128)S(1)}, f32[96,16,32]{0,2,1:T(8,128)}, u32[]{:S(2)}) copy-start(f32[96,16,32]{0,2,1:T(8,128)} %pad.443) | copy-start | bytes 589828
  745.1 202.3 %reduce-scatter.11.cloned.1.call-start = ((), (), s32[]{:S(2)}) async-start(), calls=%async_computation.11 | async-start | bytes 7077888 | tf_op jit(solution)/shard_map/reduce_scatter | solution.py:258
  751.9 18.2 %copy-start.146 = (f32[16]{0:T(128)S(1)}, f32[16]{0:T(128)}, u32[]{:S(2)}) copy-start(f32[16]{0:T(128)} %copy-done.144) | copy-start | bytes 196
  803.5 107.3 %copy-start.20 = (f32[96,16,32]{2,1,0:T(8,128)S(1)}, f32[96,16,32]{2,1,0:T(8,128)}, u32[]{:S(2)}) copy-start(f32[96,16,32]{2,1,0:T(8,128)} %copy.189) | copy-start | bytes 589828
  812.1 102.6 %copy-start.19 = (f32[96,16,32]{2,1,0:T(8,128)S(1)}, f32[96,16,32]{2,1,0:T(8,128)}, u32[]{:S(2)}) copy-start(f32[96,16,32]{2,1,0:T(8,128)} %copy.192) | copy-start | bytes 589828
  812.1 102.6 %copy-start.51 = (f32[96,32]{1,0:T(8,128)S(1)}, f32[96,32]{1,0:T(8,128)}, u32[]{:S(2)}) copy-start(f32[96,32]{1,0:T(8,128)} %copy-done.49) | copy-start | bytes 36868
  925.4 18.7 %copy-start.101 = (f32[96,32]{1,0:T(8,128)S(1)}, f32[96,32]{1,0:T(8,128)}, u32[]{:S(2)}) copy-start(f32[96,32]{1,0:T(8,128)} %get-tuple-element.80) | copy-start | bytes 36868
  925.4 18.9 %copy-start.100 = (f32[96,32]{1,0:T(8,128)S(1)}, f32[96,32]{1,0:T(8,128)}, u32[]{:S(2)}) copy-start(f32[96,32]{1,0:T(8,128)} %get-tuple-element.81) | copy-start | bytes 36868
  925.4 19.0 %copy-start.99 = (f32[96,32]{1,0:T(8,128)S(1)}, f32[96,32]{1,0:T(8,128)}, u32[]{:S(2)}) copy-start(f32[96,32]{1,0:T(8,128)} %get-tuple-element.82) | copy-start | bytes 36868
  925.4 19.0 %copy-start.98 = (f32[96,32]{1,0:T(8,128)S(1)}, f32[96,32]{1,0:T(8,128)}, u32[]{:S(2)}) copy-start(f32[96,32]{1,0:T(8,128)} %get-tuple-element.83) | copy-start | bytes 36868
  925.4 19.1 %copy-start.97 = (f32[96,32]{1,0:T(8,128)S(1)}, f32[96,32]{1,0:T(8,128)}, u32[]{:S(2)}) copy-start(f32[96,32]{1,0:T(8,128)} %get-tuple-element.84) | copy-start | bytes 36868
  925.4 19.2 %copy-start.96 = (f32[96,32]{1,0:T(8,128)S(1)}, f32[96,32]{1,0:T(8,128)}, u32[]{:S(2)}) copy-start(f32[96,32]{1,0:T(8,128)} %get-tuple-element.85) | copy-start | bytes 36868
  925.4 19.2 %copy-start.40 = (bf16[2048,96]{0,1:T(8,128)(2,1)S(1)}, bf16[2048,96]{0,1:T(8,128)(2,1)}, u32[]{:S(2)}) copy-start(bf16[2048,96]{0,1:T(8,128)(2,1)} %copy-done.38) | copy-start | bytes 1179652
  925.4 19.2 %copy-start.42 = (bf16[2048,96]{0,1:T(8,128)(2,1)S(1)}, bf16[2048,96]{0,1:T(8,128)(2,1)}, u32[]{:S(2)}) copy-start(bf16[2048,96]{0,1:T(8,128)(2,1)} %copy-done.41) | copy-start | bytes 1179652
  925.4 19.5 %copy-start.93 = (f32[96,32]{0,1:T(8,128)S(1)}, f32[96,32]{0,1:T(8,128)}, u32[]{:S(2)}) copy-start(f32[96,32]{0,1:T(8,128)} %copy-done.92) | copy-start | bytes 36868
  925.5 19.5 %copy-start.95 = (f32[96,32]{0,1:T(8,128)S(1)}, f32[96,32]{0,1:T(8,128)}, u32[]{:S(2)}) copy-start(f32[96,32]{0,1:T(8,128)} %copy-done.94) | copy-start | bytes 36868
  925.5 19.5 %copy-start.85 = (f32[96,32]{0,1:T(8,128)S(1)}, f32[96,32]{0,1:T(8,128)}, u32[]{:S(2)}) copy-start(f32[96,32]{0,1:T(8,128)} %param.38) | copy-start | bytes 36868
  925.5 19.5 %copy-start.87 = (f32[96,32]{0,1:T(8,128)S(1)}, f32[96,32]{0,1:T(8,128)}, u32[]{:S(2)}) copy-start(f32[96,32]{0,1:T(8,128)} %copy-done.86) | copy-start | bytes 36868
  925.5 19.5 %copy-start.89 = (f32[96,32]{0,1:T(8,128)S(1)}, f32[96,32]{0,1:T(8,128)}, u32[]{:S(2)}) copy-start(f32[96,32]{0,1:T(8,128)} %copy-done.88) | copy-start | bytes 36868
  925.5 19.5 %copy-start.102 = (f32[96,32]{0,1:T(8,128)S(1)}, f32[96,32]{0,1:T(8,128)}, u32[]{:S(2)}) copy-start(f32[96,32]{0,1:T(8,128)} %param.40) | copy-start | bytes 36868
  925.5 19.5 %copy-start.103 = (f32[96,32]{0,1:T(8,128)S(1)}, f32[96,32]{0,1:T(8,128)}, u32[]{:S(2)}) copy-start(f32[96,32]{0,1:T(8,128)} %param.39) | copy-start | bytes 36868
  925.5 19.5 %copy-start.104 = (f32[96,32]{0,1:T(8,128)S(1)}, f32[96,32]{0,1:T(8,128)}, u32[]{:S(2)}) copy-start(f32[96,32]{0,1:T(8,128)} %param.37) | copy-start | bytes 36868
  925.5 19.5 %copy-start.140 = (f32[96]{0:T(128)S(1)}, f32[96]{0:T(128)}, u32[]{:S(2)}) copy-start(f32[96]{0:T(128)} %copy-done.139) | copy-start | bytes 1156
  925.5 19.6 %copy-start.166 = (f32[96]{0:T(128)S(1)}, f32[96]{0:T(128)}, u32[]{:S(2)}) copy-start(f32[96]{0:T(128)} %param.36) | copy-start | bytes 1156
  945.3 34.5 %copy-start.158 = (f32[96]{0:T(128)S(1)}, f32[96]{0:T(128)}, u32[]{:S(2)}) copy-start(f32[96]{0:T(128)} %get-tuple-element.130) | copy-start | bytes 1156
  945.3 34.4 %copy-start.159 = (f32[384]{0:T(512)S(1)}, f32[384]{0:T(512)}, u32[]{:S(2)}) copy-start(f32[384]{0:T(512)} %get-tuple-element.128) | copy-start | bytes 4612
  945.3 53.0 %copy-start.82 = (f32[96,768]{1,0:T(8,128)S(1)}, f32[96,768]{1,0:T(8,128)}, u32[]{:S(2)}) copy-start(f32[96,768]{1,0:T(8,128)} %get-tuple-element.310) | copy-start | bytes 884740
  950.5 53.2 %copy-start.1 = (bf16[768,384]{1,0:T(8,128)(2,1)S(1)}, bf16[768,384]{1,0:T(8,128)(2,1)}, u32[]{:S(2)}) copy-start(bf16[768,384]{1,0:T(8,128)(2,1)} %param.46) | copy-start | bytes 1769476
  (121 other events, 586.7 us)
Sparse Core Ops, SparseCore 0:
  13.0 40.9 all-gather.4
  255.6 72.5 reduce-scatter.4
  329.9 36.6 all-gather.8
  368.6 37.1 all-gather.6
  420.4 68.6 reduce-scatter.8
  491.3 68.1 reduce-scatter.6
  563.9 36.6 all-gather.10
  745.2 93.2 all-reduce.104
  840.8 69.8 reduce-scatter.10
where the time goes:
time: 1030 us; the launch traced here: 1010 us
  local copies, waits for them, and re-layouts  299 us (29%)
  waiting for transfers between devices  286 us (28%)
  other arithmetic  208 us (20%)
  matrix products  143 us (14%)
  blocking collectives  44.4 us (4%)
  between operations  18.6 us (2%)
    pad x46, local copies, waits for them, and re-layouts, mixer_core(): lax.associative_scan(combine_states, (mult_re, mult_im, ending_re, ending...  115 us
    scatter-add x1, other arithmetic, mixer_core(): toeplitz = jnp.where(lags >= 0, kernel[:, jnp.maximum(lags, 0)], 0.0)  98.6 us
    reduce_scatter x1, waiting for transfers between devices, channel_plan(): lax.psum_scatter(jnp.dot(core_low, w_out, preferred_element_type=jnp.floa...  71.9 us
    reduce_scatter x1, waiting for transfers between devices, channel_plan(): lax.psum_scatter(jnp.dot(active_low, w_down, preferred_element_type=jnp.f...  68.3 us
    gather x2, local copies, waits for them, and re-layouts, mixer_core(): toeplitz = jnp.where(lags >= 0, kernel[:, jnp.maximum(lags, 0)], 0.0)  63.2 us
    reduce_scatter x1, waiting for transfers between devices, channel_plan(): lax.psum_scatter(jnp.einsum('tf,df->td', grad_up_low, w_up, preferred_ele...  60.9 us
    unnamed x372, local copies, waits for them, and re-layouts  46.9 us
    all_gather x1, waiting for transfers between devices, channel_plan(): gathered_two = lax.all_gather(normed_two_low, 'chan', axis=0, tiled=True)  33.8 us
  transfers between devices with their start and end apart: 9, of which 6 were waited for; matrix products, arithmetic and copies ran while one was open for 32% of the time, Pallas kernels for 0%

commit v1 on v0

v1 whole, which is shorter than its diff:
```python
import functools

import jax
import jax.numpy as jnp
from jax import lax
from jax.experimental import pallas as pl
from jax.experimental.pallas import tpu as pltpu
from jax.sharding import PartitionSpec as P

F32 = jnp.float32
BF16 = jnp.bfloat16
MODES = 32
LANES = 128
SEGS = 8
TAPS = 4
EPSILON = 1e-05
VMEM_LIMIT = 48 * 1024 * 1024
SMEM = pl.BlockSpec(memory_space=pltpu.SMEM)


def dot_nn(a, b):
    return lax.dot_general(a, b, (((1,), (0,)), ((), ())), preferred_element_type=F32)


def dot_nt(a, b):
    return lax.dot_general(a, b, (((1,), (1,)), ((), ())), preferred_element_type=F32)


def dot_tn(a, b):
    return lax.dot_general(a, b, (((0,), (0,)), ((), ())), preferred_element_type=F32)


def cmul(ar, ai, br, bi):
    return ar * br - ai * bi, ar * bi + ai * br


def fill_powers(zr, zi, pr, pi, steps):
    ar, ai = jnp.ones_like(zr), jnp.zeros_like(zi)
    pr[pl.ds(0, MODES), :] = ar
    pi[pl.ds(0, MODES), :] = ai
    for j in range(1, steps + 1):
        ar, ai = cmul(ar, ai, zr, zi)
        pr[pl.ds(j * MODES, MODES), :] = ar
        pi[pl.ds(j * MODES, MODES), :] = ai
    return ar, ai


def over_chunk(ar, ai):
    n = 1
    while n < SEGS:
        ar, ai = cmul(ar, ai, ar, ai)
        n *= 2
    return ar, ai


def fill_kern(wr, wi, pr, pi, kern, steps):
    for j in range(steps):
        v = wr * pr[pl.ds(j * MODES, MODES), :] - wi * pi[pl.ds(j * MODES, MODES), :]
        kern[pl.ds(j, 1), :] = 2.0 * jnp.sum(v, axis=0, keepdims=True)


def row(ref, i):
    return jnp.broadcast_to(ref[pl.ds(i, 1), :], (SEGS, LANES))


def group(ref, t):
    return ref[pl.ds(t * SEGS, SEGS), :]


def sublanes():
    return lax.broadcasted_iota(jnp.int32, (SEGS, LANES), 0)


def seg_mask(keep0, keep4):
    ids = sublanes()
    m = jnp.where(ids == 0, keep0, 1.0)
    return jnp.where(ids == SEGS // 2, keep4, m)


def at_seg(ref, k):
    return ref[pl.ds(k, MODES, stride=SEGS), :]


def store_pairs(ref, values, base=0):
    for t in range(0, len(values), 2):
        ref[pl.ds(base + t * SEGS, 2 * SEGS), :] = jnp.concatenate(values[t : t + 2]).astype(BF16)


def before_kernel(
    steps, keeps, key, halo, value, taps, zr, zi,
    prod, shifted, er, ei, dr, di, halos, own, chip, pr, pi, last,
):
    c = pl.program_id(1)
    k0, k4 = keeps[c, 0], keeps[c, 1]
    mask = seg_mask(k0, k4)
    ids = sublanes()
    ar, ai = fill_powers(zr[...], zi[...], pr, pi, steps)

    @pl.when(c == 0)
    def _():
        halos[...] = halo[...]

    @pl.when(c == 1)
    def _():
        halos[...] = last[...]

    window = []
    for back in (1, 2, 3):
        v = pltpu.roll(group(key, steps - back), 1, 0)
        window.append(jnp.where(ids == 0, row(halos, SEGS - back), v) * mask)
        last[pl.ds(SEGS - back, 1), :] = v[0:1, :]
    tap = [row(taps, j) for j in range(TAPS)]
    xs = []
    for t in range(steps):
        cur = group(key, t)
        s = tap[0] * cur + tap[1] * window[0] + tap[2] * window[1] + tap[3] * window[2]
        window = [cur] + window[:2]
        shifted[pl.ds(t * SEGS, SEGS), :] = s
        p = s * group(value, t)
        prod[pl.ds(t * SEGS, SEGS), :] = p
        xs.append(p)

    def per_mode(m, carry):
        sr = si = tr = ti = jnp.zeros((SEGS, LANES), F32)
        for t in range(steps):
            j = steps - 1 - t
            sr = sr + row(pr, j * MODES + m) * xs[t]
            si = si + row(pi, j * MODES + m) * xs[t]
            if t < steps - 1:
                tr = tr + sr
                ti = ti + si
        at = pl.multiple_of(m * SEGS, SEGS)
        er[pl.ds(at, SEGS), :] = sr
        ei[pl.ds(at, SEGS), :] = si
        dr[pl.ds(at, SEGS), :] = tr
        di[pl.ds(at, SEGS), :] = ti
        return carry

    lax.fori_loop(0, MODES, per_mode, 0)
    sr = si = jnp.zeros((MODES, LANES), F32)
    for k in range(SEGS):
        if k == SEGS // 2:
            sr, si = sr * k4, si * k4
        cr, ci = cmul(sr, si, ar, ai)
        sr = cr + at_seg(er, k)
        si = ci + at_seg(ei, k)

    @pl.when(c == 0)
    def _():
        own[pl.ds(0, MODES), :] = sr
        own[pl.ds(MODES, MODES), :] = si

    @pl.when(c == 1)
    def _():
        br, bi = over_chunk(ar, ai)
        cr, ci = cmul(own[pl.ds(0, MODES), :], own[pl.ds(MODES, MODES), :], br, bi)
        keep = k0 * k4
        chip[pl.ds(0, MODES), :] = (cr * keep + sr).astype(BF16)
        chip[pl.ds(MODES, MODES), :] = (ci * keep + si).astype(BF16)


def incoming(ref_list, masks, which, ar, ai):
    br, bi = cmul(ar, ai, ar, ai)
    read = lambda r: (r[pl.ds(0, MODES), :].astype(F32), r[pl.ds(MODES, MODES), :].astype(F32))
    sr, si = read(ref_list[-1])
    for by in range(len(ref_list) - 1, 0, -1):
        m = masks[which, by]
        cr, ci = cmul(sr, si, br * m, bi * m)
        rr, ri = read(ref_list[by - 1])
        sr, si = cr + rr, ci + ri
    return sr, si


def conv_kernel(steps, n_recv, keeps, masks, x, query, er, ei, own, *refs):
    recv, (zr, zi, wr, wi, skip, conv, core, state_r, state_i, pr, pi, kern) = refs[:n_recv], refs[n_recv:]
    c = pl.program_id(1)
    k4 = keeps[c, 1]
    ar, ai = fill_powers(zr[...], zi[...], pr, pi, steps)
    fill_kern(wr[...], wi[...], pr, pi, kern, steps)
    br, bi = over_chunk(ar, ai)
    sr, si = incoming(recv, masks, 0, br, bi)
    sr, si = sr * keeps[0, 0], si * keeps[0, 0]
    cr, ci = cmul(sr, si, br * keeps[0, 1], bi * keeps[0, 1])
    cr = (cr + own[pl.ds(0, MODES), :]) * keeps[1, 0]
    ci = (ci + own[pl.ds(MODES, MODES), :]) * keeps[1, 0]
    sr, si = jnp.where(c == 0, sr, cr), jnp.where(c == 0, si, ci)
    for k in range(SEGS):
        if k == SEGS // 2:
            sr, si = sr * k4, si * k4
        state_r[pl.ds(k, MODES, stride=SEGS), :] = sr
        state_i[pl.ds(k, MODES, stride=SEGS), :] = si
        if k < SEGS - 1:
            cr, ci = cmul(sr, si, ar, ai)
            sr = cr + at_seg(er, k)
            si = ci + at_seg(ei, k)
    sk = row(skip, 0)
    ys = [sk * group(x, t) for t in range(steps)]
    for j in range(steps):
        kj = row(kern, j)
        for t in range(j, steps):
            ys[t] = ys[t] + kj * group(x, t - j)

    def per_mode(m, ys):
        at = pl.multiple_of(m * SEGS, SEGS)
        a, b = state_r[pl.ds(at, SEGS), :], state_i[pl.ds(at, SEGS), :]
        u, v = cmul(2.0 * row(wr, m), 2.0 * row(wi, m), a, b)
        return tuple(
            y + (row(pr, (t + 1) * MODES + m) * u - row(pi, (t + 1) * MODES + m) * v) for t, y in enumerate(ys)
        )

    ys = lax.fori_loop(0, MODES, per_mode, tuple(ys))
    low = []
    for t in range(steps):
        conv[pl.ds(t * SEGS, SEGS), :] = ys[t]
        low.append(ys[t] * group(query, t))
    store_pairs(core, low)


def after_kernel(
    steps, keeps, grad_core, query, conv, zr, zi, wr, wi,
    g, grad_query, qr, qi, rr, ri, own, chip, pr, pi,
):
    c = 1 - pl.program_id(1)
    k0, k4 = keeps[c, 0], keeps[c, 1]
    ar, ai = fill_powers(zr[...], zi[...], pr, pi, steps)
    gs, low = [], []
    for t in range(steps):
        d = group(grad_core, t)
        v = d * group(query, t)
        g[pl.ds(t * SEGS, SEGS), :] = v
        gs.append(v)
        low.append(d * group(conv, t))
    store_pairs(grad_query, low)

    def per_mode(m, carry):
        sr = si = tr = ti = jnp.zeros((SEGS, LANES), F32)
        for t in reversed(range(steps)):
            sr = sr + row(pr, (t + 1) * MODES + m) * gs[t]
            si = si + row(pi, (t + 1) * MODES + m) * gs[t]
            tr = tr + sr
            ti = ti + si
        at = pl.multiple_of(m * SEGS, SEGS)
        qr[pl.ds(at, SEGS), :] = sr
        qi[pl.ds(at, SEGS), :] = si
        rr[pl.ds(at, SEGS), :] = tr
        ri[pl.ds(at, SEGS), :] = ti
        return carry

    lax.fori_loop(0, MODES, per_mode, 0)
    w2r, w2i = 2.0 * wr[...], 2.0 * wi[...]
    lr = jnp.where(c == 1, 0.0, own[pl.ds(0, MODES), :])
    li = jnp.where(c == 1, 0.0, own[pl.ds(MODES, MODES), :])
    for k in reversed(range(SEGS)):
        cr, ci = cmul(lr, li, ar, ai)
        ur, ui = cmul(w2r, w2i, at_seg(qr, k), at_seg(qi, k))
        lr, li = ur + cr, ui + ci
        if k == SEGS // 2:
            lr, li = lr * k4, li * k4
    lr, li = lr * k0, li * k0

    @pl.when(c == 1)
    def _():
        own[pl.ds(0, MODES), :] = lr
        own[pl.ds(MODES, MODES), :] = li

    @pl.when(c == 0)
    def _():
        chip[pl.ds(0, MODES), :] = lr.astype(BF16)
        chip[pl.ds(MODES, MODES), :] = li.astype(BF16)


def grads_kernel(steps, n_recv, keeps, masks, g, x, qr, qi, rr, ri, state_r, state_i, dr, di, own, *refs):
    recv = refs[:n_recv]
    zr, zi, wr, wi, skip, taps, key, halos, value, shifted = refs[n_recv : n_recv + 10]
    grad_kv, ghalo, dwr, dwi, dzr, dzi, dskip, dtaps, pr, pi, kern, mur, mui, nexts = refs[n_recv + 10 :]
    c = 1 - pl.program_id(1)
    lane = pl.program_id(0)
    k0, k4 = keeps[c, 0], keeps[c, 1]
    mask = seg_mask(k0, k4)
    ids = sublanes()
    ar, ai = fill_powers(zr[...], zi[...], pr, pi, steps)
    w2r, w2i = 2.0 * wr[...], 2.0 * wi[...]
    fill_kern(wr[...], wi[...], pr, pi, kern, steps)
    br, bi = over_chunk(ar, ai)
    mr, mi = incoming(recv, masks, 1, br, bi)
    keep = keeps[1, 0] * keeps[1, 1]
    cr, ci = cmul(mr, mi, br * keep, bi * keep)
    cr, ci = cr + own[pl.ds(0, MODES), :], ci + own[pl.ds(MODES, MODES), :]
    mr, mi = jnp.where(c == 1, mr, cr), jnp.where(c == 1, mi, ci)
    zero = jnp.zeros((MODES, LANES), F32)
    awr = awi = azr = azi = acr = aci = zero
    for k in reversed(range(SEGS)):
        mur[pl.ds(k, MODES, stride=SEGS), :] = mr
        mui[pl.ds(k, MODES, stride=SEGS), :] = mi
        s_r, s_i = at_seg(state_r, k), at_seg(state_i, k)
        q_r, q_i = at_seg(qr, k), at_seg(qi, k)
        u = cmul(s_r, s_i, q_r, q_i)
        awr, awi = awr + u[0], awi + u[1]
        u = cmul(s_r, s_i, at_seg(rr, k), at_seg(ri, k))
        azr, azi = azr + u[0], azi + u[1]
        u = cmul(mr, mi, at_seg(dr, k), at_seg(di, k))
        acr, aci = acr + u[0], aci + u[1]
        u = cmul(mr, mi, s_r, s_i)
        u = cmul(u[0], u[1], ar, ai)
        acr, aci = acr + float(steps) * u[0], aci + float(steps) * u[1]
        if k > 0:
            ur, ui = cmul(w2r, w2i, q_r, q_i)
            cr, ci = cmul(mr, mi, ar, ai)
            mr, mi = ur + cr, ui + ci
            if k == SEGS // 2:
                mr, mi = mr * k4, mi * k4
    for j in range(steps):
        acc = group(g, j) * group(x, 0)
        for t in range(j + 1, steps):
            acc = acc + group(g, t) * group(x, t - j)
        lag = jnp.sum(acc, axis=0, keepdims=True)
        u, v = pr[pl.ds(j * MODES, MODES), :] * lag, pi[pl.ds(j * MODES, MODES), :] * lag
        awr, awi = awr + u, awi + v
        azr, azi = azr + float(j) * u, azi + float(j) * v
    u = cmul(w2r, w2i, azr, azi)
    sk = row(skip, 0)
    gx = []
    dsk = jnp.zeros((SEGS, LANES), F32)
    for t in range(steps):
        gt = group(g, t)
        dsk = dsk + gt * group(x, t)
        gx.append(sk * gt)
    for j in range(steps):
        kj = row(kern, j)
        for t in range(0, steps - j):
            gx[t] = gx[t] + kj * group(g, t + j)

    def per_mode(m, gx):
        a = pl.multiple_of(m * SEGS, SEGS)
        u, v = mur[pl.ds(a, SEGS), :], mui[pl.ds(a, SEGS), :]
        return tuple(
            y + (row(pr, (steps - 1 - t) * MODES + m) * u - row(pi, (steps - 1 - t) * MODES + m) * v)
            for t, y in enumerate(gx)
        )

    gx = list(lax.fori_loop(0, MODES, per_mode, tuple(gx)))
    gv = [gx[t] * group(shifted, t) for t in range(steps)]
    gs = [gx[t] * group(value, t) for t in range(steps)]
    tap = [row(taps, j) for j in range(TAPS)]
    window = []
    for back in (1, 2, 3):
        v = pltpu.roll(group(key, steps - back), 1, 0)
        window.append(jnp.where(ids == 0, row(halos, SEGS - back), v) * mask)
    acc = [jnp.zeros((SEGS, LANES), F32)] * TAPS
    for t in range(steps):
        cur = group(key, t)
        for j, v in enumerate([cur] + window):
            acc[j] = acc[j] + gs[t] * v
        window = [cur] + window[:2]
    new = [2.0 * awr, -2.0 * awi, u[0] + acr, -(u[1] + aci), jnp.sum(dsk, axis=0, keepdims=True)]
    new.append(jnp.concatenate([jnp.sum(a, axis=0, keepdims=True) for a in acc], axis=0))
    outs = [dwr, dwi, dzr, dzi, dskip, dtaps]

    @pl.when(c == 1)
    def _():
        nexts[...] = jnp.zeros_like(nexts)
        for ref, v in zip(outs, new):
            ref[...] = v

    @pl.when(c == 0)
    def _():
        for ref, v in zip(outs, new):
            ref[...] += v

    begin = [gs[t] * mask for t in range(TAPS - 1)]
    later = [
        pltpu.roll(jnp.where(ids == 0, group(nexts, t), v), SEGS - 1, 0) for t, v in enumerate(begin)
    ]
    for t, v in enumerate(begin):
        nexts[pl.ds(t * SEGS, SEGS), :] = v
    ext = gs + later
    gk = [tap[0] * ext[t] + tap[1] * ext[t + 1] + tap[2] * ext[t + 2] + tap[3] * ext[t + 3] for t in range(steps)]
    size = steps * SEGS
    for part, values in enumerate((gk, gv)):
        at = pl.multiple_of((part * pl.num_programs(0) + lane) * LANES, LANES)
        for t in range(0, steps, 2):
            r = pl.multiple_of(c * size + t * SEGS, 2 * SEGS)
            grad_kv[pl.ds(r, 2 * SEGS), pl.ds(at, LANES)] = jnp.concatenate(values[t : t + 2]).astype(BF16)
    rows = [jnp.zeros((SEGS - TAPS + 1, LANES), F32)]
    for back in (3, 2, 1):
        v = jnp.zeros((1, LANES), F32)
        for j in range(back, TAPS):
            v = v + taps[pl.ds(j, 1), :] * begin[j - back][0:1, :]
        rows.append(v)
    ghalo[...] = jnp.concatenate(rows, axis=0)


class Mixer:
    def __init__(self, rows, channels):
        self.rows, self.channels, self.steps = rows, channels, rows // SEGS
        self.lanes = channels // LANES

    def chunk(self, rows, shift=0, flip=False):
        if flip:
            return pl.BlockSpec((rows, LANES), lambda l, c: (1 - c, l + shift))
        return pl.BlockSpec((rows, LANES), lambda l, c: (c, l + shift))

    def fixed(self, rows, at=0):
        return pl.BlockSpec((rows, LANES), lambda l, c: (at, l))

    def shape(self, rows, kind=F32):
        return jax.ShapeDtypeStruct((rows, self.channels), kind)

    def call(self, name, kernel, in_specs, out_specs, out_shape, scratch, work):
        table = pltpu.VMEM(((self.steps + 1) * MODES, LANES), F32)
        return pl.pallas_call(
            kernel,
            grid=(self.lanes, 2),
            in_specs=in_specs,
            out_specs=out_specs,
            out_shape=out_shape,
            scratch_shapes=[table, table] + scratch,
            compiler_params=pltpu.CompilerParams(vmem_limit_bytes=VMEM_LIMIT),
            cost_estimate=pl.CostEstimate(flops=work, bytes_accessed=work // 400, transcendentals=0),
            name=name,
        )

    def before(self, keeps, key_value, taps, zr, zi):
        n, ms = self.rows, MODES * SEGS
        big, states = self.chunk(n), self.chunk(ms)
        return self.call(
            "ssm_before",
            functools.partial(before_kernel, self.steps),
            [SMEM, big, self.fixed(SEGS, 2 * n // SEGS), self.chunk(n, self.lanes), self.fixed(TAPS)]
            + [self.fixed(MODES)] * 2,
            [big, big] + [states] * 4 + [self.chunk(SEGS), self.fixed(2 * MODES), self.fixed(2 * MODES)],
            [self.shape(2 * n)] * 2 + [self.shape(2 * ms)] * 4
            + [self.shape(2 * SEGS), self.shape(2 * MODES), self.shape(2 * MODES, BF16)],
            [pltpu.VMEM((SEGS, LANES), F32)],
            10**10,
        )(keeps, key_value, key_value, key_value, taps, zr, zi)

    def conv(self, keeps, masks, prod, query, er, ei, own, recv, zr, zi, wr, wi, skip):
        n, ms = self.rows, MODES * SEGS
        big, states, ends, modes = self.chunk(n), self.chunk(ms), self.fixed(2 * MODES), self.fixed(MODES)
        return self.call(
            "ssm_conv",
            functools.partial(conv_kernel, self.steps, len(recv)),
            [SMEM, SMEM, big, big, states, states] + [ends] * (1 + len(recv)) + [modes] * 4 + [self.fixed(1)],
            [big, big, states, states],
            [self.shape(2 * n), self.shape(2 * n, BF16)] + [self.shape(2 * ms)] * 2,
            [pltpu.VMEM((self.steps, LANES), F32)],
            10**10,
        )(keeps, masks, prod, query, er, ei, own, *recv, zr, zi, wr, wi, skip)

    def after(self, keeps, grad_core, query, conv, zr, zi, wr, wi):
        n, ms = self.rows, MODES * SEGS
        big, states, modes = self.chunk(n, 0, True), self.chunk(ms, 0, True), self.fixed(MODES)
        ends = self.fixed(2 * MODES)
        return self.call(
            "ssm_after",
            functools.partial(after_kernel, self.steps),
            [SMEM, big, big, big] + [modes] * 4,
            [big, big] + [states] * 4 + [ends, ends],
            [self.shape(2 * n), self.shape(2 * n, BF16)] + [self.shape(2 * ms)] * 4
            + [self.shape(2 * MODES), self.shape(2 * MODES, BF16)],
            [],
            10**10,
        )(keeps, grad_core, query, conv, zr, zi, wr, wi)

    def grads(self, keeps, masks, g, prod, q, state, d, own, recv, zr, zi, wr, wi, skip, taps, key_value, halos, shifted):
        n, ms = self.rows, MODES * SEGS
        big, states, modes = self.chunk(n, 0, True), self.chunk(ms, 0, True), self.fixed(MODES)
        ends, one, four = self.fixed(2 * MODES), self.fixed(1), self.fixed(TAPS)
        return self.call(
            "ssm_grads",
            functools.partial(grads_kernel, self.steps, len(recv)),
            [SMEM, SMEM, big, big] + [states] * 8 + [ends] * (1 + len(recv)) + [modes] * 4
            + [one, four, big, self.chunk(SEGS, 0, True), self.chunk(n, self.lanes, True), big],
            [pl.BlockSpec((2 * n, 2 * self.channels), lambda l, c: (0, 0)), self.fixed(SEGS)] + [modes] * 4 + [one, four],
            [jax.ShapeDtypeStruct((2 * n, 2 * self.channels), BF16), self.shape(SEGS)]
            + [self.shape(MODES)] * 4 + [self.shape(1), self.shape(TAPS)],
            [pltpu.VMEM((self.steps, LANES), F32)] + [pltpu.VMEM((ms, LANES), F32)] * 2
            + [pltpu.VMEM(((TAPS - 1) * SEGS, LANES), F32)],
            15 * 10**9,
        )(keeps, masks, g, prod, *q, *state, *d, own, *recv, zr, zi, wr, wi, skip, taps, key_value, halos, key_value, shifted)


TILE = 128


def feed_forward_kernel(n_sets, up_at, down_at, *refs):
    x_own, x_sib, c_own, c_sib = refs[:4]
    ups, downs = refs[4 : 4 + n_sets], refs[4 + n_sets : 4 + 2 * n_sets]
    bias = refs[4 + 2 * n_sets]
    outs = refs[5 + 2 * n_sets :]
    branch, grad_x, grad_bias = outs[0:2], outs[2:4], outs[4]
    n_up = 1 + max(a for a, _ in up_at)
    up_refs = outs[5 : 5 + n_up]
    down_refs = outs[5 + n_up : -4]
    xs, cs, acts, backs = outs[-4:]
    half = x_own.shape[0]
    xs[pl.ds(0, half), :] = x_own[...]
    xs[pl.ds(half, half), :] = x_sib[...]
    cs[pl.ds(0, half), :] = c_own[...]
    cs[pl.ds(half, half), :] = c_sib[...]
    for s in range(n_sets):
        up, down = ups[s], downs[s]
        total = None
        for r in range(2 * half // TILE):
            at = pl.ds(r * TILE, TILE)
            side, place = r * TILE // half, pl.ds(r * TILE % half, TILE)
            v = dot_nt(xs[at, :], up[...]) + bias[pl.ds(s, 1), :]
            square = v * v
            th = jnp.tanh(v * (0.79788456 + 0.79788456 * 0.044715 * square))
            half_up = 0.5 + 0.5 * th
            slope = half_up + v * (0.5 - 0.5 * th * th) * (0.79788456 + 0.79788456 * 3.0 * 0.044715 * square)
            active = (v * half_up).astype(BF16)
            back = (dot_nt(cs[at, :], down[...]) * slope).astype(BF16)
            acts[at, :] = active
            backs[at, :] = back
            part = jnp.sum(back.astype(F32), axis=0, keepdims=True)
            total = part if total is None else total + part
            out, grad = dot_nn(active, down[...]), dot_nn(back, up[...])
            if s == 0:
                branch[side][place, :] = out
                grad_x[side][place, :] = grad
            else:
                branch[side][place, :] += out
                grad_x[side][place, :] += grad
        grad_bias[pl.ds(s, 1), :] = total
        array, slot = up_at[s]
        up_refs[array][slot] = dot_tn(backs[...], xs[...]).astype(BF16)
        array, slot = down_at[s]
        down_refs[array][slot] = dot_tn(acts[...], cs[...]).astype(BF16)


def feed_forward(x_own, x_sib, c_own, c_sib, ups, downs, bias, up_at, down_at):
    rows, width = x_own.shape
    units = bias.shape[1]

    def arrays(where):
        return [
            jax.ShapeDtypeStruct((sum(a == i for a, _ in where), units, width), BF16)
            for i in range(1 + max(a for a, _ in where))
        ]

    full = jax.ShapeDtypeStruct((rows, width), F32)
    n_up = 1 + max(a for a, _ in up_at)
    out = pl.pallas_call(
        functools.partial(feed_forward_kernel, len(ups), up_at, down_at),
        out_shape=[full] * 4 + [jax.ShapeDtypeStruct(bias.shape, F32)] + arrays(up_at) + arrays(down_at),
        scratch_shapes=[pltpu.VMEM((2 * rows, width), BF16)] * 2 + [pltpu.VMEM((2 * rows, units), BF16)] * 2,
        compiler_params=pltpu.CompilerParams(vmem_limit_bytes=VMEM_LIMIT),
        cost_estimate=pl.CostEstimate(
            flops=24 * rows * width * units * len(ups), bytes_accessed=12 * units * width * len(ups), transcendentals=0
        ),
        name="feed_forward",
    )(x_own, x_sib, c_own, c_sib, *ups, *downs, bias)
    return out[0:2], out[2:4], out[4], out[5 : 5 + n_up], out[5 + n_up :]


def normalize(values):
    center = values - jnp.mean(values, axis=-1, keepdims=True)
    scale = lax.rsqrt(jnp.mean(center * center, axis=-1, keepdims=True) + EPSILON)
    return center * scale, scale


def normalize_back(grad, gain, xhat, scale):
    gy = grad * gain
    mean_gy = jnp.mean(gy, axis=-1, keepdims=True)
    mean_gx = jnp.mean(gy * xhat, axis=-1, keepdims=True)
    return scale * (gy - mean_gy - xhat * mean_gx)


def ssm_tables(log_step, log_decay, frequency, out_real, out_imag):
    step_size = jnp.exp(log_step)
    rate = -jnp.exp(log_decay)
    decay = rate * step_size
    turn = frequency * step_size
    growth = jnp.exp(decay)
    ratio_re = growth * jnp.cos(turn) - 1.0
    ratio_im = growth * jnp.sin(turn)
    denom = rate * rate + frequency * frequency
    scaled_re = (ratio_re * rate + ratio_im * frequency) / denom
    scaled_im = (ratio_im * rate - ratio_re * frequency) / denom
    weight_re = out_real * scaled_re - out_imag * scaled_im
    weight_im = out_real * scaled_im + out_imag * scaled_re
    return decay, turn, weight_re, weight_im


def local(
    groups, chips,
    hidden_in, mix_gain, mix_shift, w_query, bias_query, w_key, bias_key, w_value, bias_value, shift_taps,
    log_step, log_decay, frequency, out_real, out_imag, skip_gain, w_out, bias_out, mlp_gain, mlp_shift,
    w_up, bias_up, w_down, bias_down, cotangent, seq_blocks,
):
    rows, width = hidden_in.shape
    shard, shard_units = w_query.shape[1], w_up.shape[1]
    chans, channels = 2 * chips, chips * shard
    cut, unit_cut = shard // groups, shard_units // groups
    steps = rows // SEGS
    me_group, me_chan = lax.axis_index("group"), lax.axis_index("chan")
    me_chip, me_core = me_chan // 2, me_chan % 2
    same_core = [[2 * z + k for z in range(chips)] for k in range(2)]
    square = groups == 4

    def swap(x, axis, members=None):
        return lax.all_to_all(x, axis, 0, 0, axis_index_groups=members, tiled=True)

    def spread(x, axis, count, members=None):
        return swap(jnp.broadcast_to(x[None], (count,) + x.shape), axis, members)

    def along_z(x):
        return spread(x, "chan", chips, same_core)

    def fold_z(x):
        return jnp.sum(swap(x, "chan", same_core).astype(F32), axis=0)

    def group_swap(x, bit):
        return lax.ppermute(x, "group", [(i, i ^ bit) for i in range(groups)])

    def sibling(x):
        return lax.ppermute(x, "chan", [(i, i ^ 1) for i in range(chans)])

    def chip_shift(x, by):
        pairs = [(i, i + 2 * by) for i in range(chans) if 0 <= i + 2 * by < chans]
        return lax.ppermute(x, "chan", pairs)

    def gather_groups(a, b):
        if not square:
            return [list(spread(x, "group", groups)) for x in (a, b)]
        ax, bx, ay, by = group_swap(a, 1), group_swap(b, 1), group_swap(a, 2), group_swap(b, 2)
        return [a, ax, ay, group_swap(ay, 1)], [b, bx, by, group_swap(bx, 2)]

    def by_group(x, axis):
        if not square:
            return x
        pick = lambda order: jnp.concatenate([lax.slice_in_dim(x, i, i + 1, axis=axis) for i in order], axis=axis)
        for bit, order in ((1, (1, 0, 3, 2)), (2, (2, 3, 0, 1))):
            x = jnp.where((me_group & bit) > 0, pick(order), x)
        return x

    def add(*xs):
        return sum(x.astype(F32) for x in xs).astype(BF16)

    def fold_pair(send_a, a0, ay, send_b, b0, bx):
        ra, rb = group_swap(send_a, 1), group_swap(send_b, 2)
        ra2, rb2 = group_swap(add(ay, ra[1]), 2), group_swap(add(bx, rb[1]), 1)
        return add(a0, ra[0], ra2), add(b0, rb[0], rb2)

    def fold_groups(a, b):
        if not square:
            return [jnp.sum(swap(x, "group").astype(F32), axis=0).astype(BF16) for x in (a, b)]
        pair = lambda x, i, j: jnp.stack([x[i], x[j]])
        return fold_pair(pair(a, 1, 3), a[0], a[2], pair(b, 2, 3), b[0], b[1])

    def share(x):
        return lax.dynamic_index_in_dim(x.reshape(groups, -1, width), me_group, 0, keepdims=False)

    def to_steps(x):
        return x.reshape(SEGS, steps, width).transpose(1, 0, 2).reshape(rows, width)

    def to_rows(x):
        return x.reshape(steps, SEGS, width).transpose(1, 0, 2).reshape(rows, width)

    def in_chunks(own, other):
        return jnp.where(me_core == 0, own, other), jnp.where(me_core == 0, other, own)

    kv_piece = jnp.stack([share(w_key.T), share(w_value.T)])
    qo_piece = jnp.stack([share(w_query.T), share(w_out)])
    kv_z = along_z(kv_piece)
    small = jnp.concatenate(
        [
            log_decay.T, frequency.T, out_real.T, out_imag.T, shift_taps.T,
            jnp.stack([log_step, skip_gain, bias_query, bias_key, bias_value]),
            bias_up.reshape(shard_units // shard, shard),
        ]
    )
    small = along_z(small)
    qo_z = along_z(qo_piece)
    up_z = along_z(share(w_up.T))
    down_z = along_z(share(w_down))
    n_small = 4 * MODES + TAPS + 5
    units_bias = by_group(small[:, n_small:].reshape(chips, groups, unit_cut), 1)
    units_bias = jnp.moveaxis(units_bias, 1, 0).reshape(groups, chips * unit_cut)
    small = by_group(small[:, :n_small].reshape(chips, n_small, groups, cut), 2)
    small = jnp.transpose(small, (1, 2, 0, 3)).reshape(n_small, channels)
    all_decay, all_freq, all_real, all_imag = (small[i * MODES : (i + 1) * MODES] for i in range(4))
    rest = small[4 * MODES :]
    all_taps, all_step, all_skip = rest[:TAPS], rest[TAPS : TAPS + 1], rest[TAPS + 1 : TAPS + 2]
    all_bias = rest[TAPS + 2 :]

    def whole(parts):
        return jnp.concatenate([p.reshape(-1, width) for p in parts])

    ks, vs = gather_groups(kv_z[:, 0], kv_z[:, 1])
    wkv = whole(ks + vs)
    qs, os_ = gather_groups(qo_z[:, 0], qo_z[:, 1])
    wq, wo = whole(qs), whole(os_)
    ups, downs = gather_groups(up_z, down_z)
    ups, downs = ([p.reshape(-1, width) for p in x] for x in (ups, downs))

    first = seq_blocks[0, 0]
    second = first + seq_blocks[0, 1]

    def keep(block):
        starts = (block == 0) | (block == first) | (block == second)
        return jnp.where(starts, 0.0, 1.0).astype(F32)

    blocks = 4 * me_chip + jnp.arange(4)
    keeps = keep(blocks).reshape(2, 2)
    near = me_chip + jnp.stack([-jnp.arange(chips), jnp.arange(chips)])
    masks = jnp.prod(keep(4 * near[..., None] + jnp.arange(4)), axis=-1)

    halo_in = lax.ppermute(hidden_in[rows - SEGS :], "chan", [(2 * z + 1, 2 * z + 3) for z in range(chips - 1)])
    inputs = jnp.concatenate([to_steps(hidden_in), halo_in]).astype(F32)
    xhat, scale = normalize(inputs)
    normed = (xhat * mix_gain + mix_shift).astype(BF16)
    normed_sib = sibling(normed)
    chunk_0, chunk_1 = in_chunks(normed[:rows], normed_sib[:rows])
    halo = jnp.where(me_core == 0, normed_sib[rows:], normed[rows:])
    normed_all = jnp.concatenate([chunk_0, chunk_1, halo])
    key_value = dot_nt(normed_all, wkv) + all_bias[1:3].reshape(-1)
    query = dot_nt(normed_all[: 2 * rows], wq) + all_bias[0]

    (decay, turn, wr, wi), tables_back = jax.vjp(ssm_tables, all_step, all_decay, all_freq, all_real, all_imag)
    mag = jnp.exp(decay)
    zr, zi = mag * jnp.cos(turn), mag * jnp.sin(turn)
    mixer = Mixer(rows, channels)
    prod, shifted, er, ei, dr, di, halos, end_0, end = mixer.before(keeps, key_value, all_taps, zr, zi)
    recv = [chip_shift(end, by) for by in range(1, chips)]
    conv, core_low, state_r, state_i = mixer.conv(
        keeps, masks, prod, query, er, ei, end_0, recv, zr, zi, wr, wi, all_skip
    )
    core_own, core_other = in_chunks(core_low[:rows], core_low[rows:])
    from_sib = sibling(dot_nn(core_other, wo))
    residual = inputs[:rows] + dot_nn(core_own, wo) + from_sib + bias_out
    xhat_two, scale_two = normalize(residual)
    normed_two = (xhat_two * mlp_gain + mlp_shift).astype(BF16)
    cot = to_steps(cotangent)
    outgoing = cot.astype(F32)
    if square:
        up_at, down_at = ((0, 0), (2, 0), (1, 0), (2, 1)), ((0, 0), (1, 0), (2, 0), (2, 1))
    else:
        up_at = down_at = tuple((0, s) for s in range(groups))
    branch, grad_two, grad_units_bias, grad_ups, grad_downs = feed_forward(
        normed_two, sibling(normed_two), cot, sibling(cot), ups, downs, units_bias, up_at, down_at
    )
    output = to_rows((residual + branch[0] + sibling(branch[1]) + bias_down).astype(BF16))
    if square:
        ff = fold_pair(
            grad_ups[2], grad_ups[0][0], grad_ups[1][0], grad_downs[2], grad_downs[0][0], grad_downs[1][0]
        )
    else:
        ff = fold_groups(grad_ups[0], grad_downs[0])
    ff = jnp.stack([x.reshape(chips, unit_cut, width) for x in ff], axis=1)
    ff = fold_z(ff).astype(BF16)
    ff = spread(ff, "group", groups).astype(F32)
    ff = jnp.moveaxis(ff, 1, 0).reshape(2, shard_units, width)

    grad_two = grad_two[0] + sibling(grad_two[1])
    grad_residual = outgoing + normalize_back(grad_two, mlp_gain, xhat_two, scale_two)
    grad_res_low = grad_residual.astype(BF16)
    grad_res_all = jnp.concatenate(in_chunks(grad_res_low, sibling(grad_res_low)))
    grad_core = dot_nt(grad_res_all, wo)
    grad_wo = dot_tn(core_low, grad_res_all)
    g, grad_query, *qsums, back_1, back = mixer.after(keeps, grad_core, query, conv, zr, zi, wr, wi)
    recv = [chip_shift(back, -by) for by in range(1, chips)]
    grad_wq = dot_tn(grad_query, normed_all[: 2 * rows])
    grad_kv, grad_halo, dwr, dwi, dzr, dzi, dskip, dtaps = mixer.grads(
        keeps, masks, g, prod, qsums, (state_r, state_i), (dr, di), back_1, recv, zr, zi, wr, wi, all_skip, all_taps,
        key_value, halos, shifted,
    )
    dstep, ddecay, dfreq, dreal, dimag = tables_back((dzr, dzi, dwr, dwi))
    grad_halo = grad_halo.astype(BF16)
    grad_wkv = dot_tn(grad_kv, normed_all[: 2 * rows])
    grad_wk = grad_wkv[:channels] + dot_tn(grad_halo, normed_all[2 * rows :])
    grad_wv = grad_wkv[channels:]
    kv_own, kv_other = in_chunks(grad_kv[:rows], grad_kv[rows:])
    q_own, q_other = in_chunks(grad_query[:rows], grad_query[rows:])
    halo_back = dot_nn(grad_halo, wkv[:channels])
    to_sib = jnp.concatenate([dot_nn(kv_other, wkv) + dot_nn(q_other, wq), halo_back])
    from_sib = sibling(to_sib)
    halo_back = lax.ppermute(
        halo_back + from_sib[rows:], "chan", [(2 * z + 3, 2 * z + 1) for z in range(chips - 1)]
    )
    grad_normed = dot_nn(kv_own, wkv) + dot_nn(q_own, wq) + from_sib[:rows]
    grad_normed = grad_normed.reshape(steps, SEGS, width)
    grad_normed = grad_normed.at[steps - SEGS :, SEGS - 1].add(halo_back).reshape(rows, width)
    grad_inputs = grad_residual + normalize_back(grad_normed, mix_gain, xhat[:rows], scale[:rows])
    grad_input = to_rows(grad_inputs.astype(BF16))

    col = lambda x: jnp.sum(x.astype(F32), axis=0)
    features = jnp.stack(
        [
            col(grad_normed * xhat[:rows]), col(grad_normed), col(grad_residual),
            col(grad_two * xhat_two), col(grad_two), col(outgoing),
        ]
    )
    features = features.reshape(6, chips, 2, shard)
    mine = lambda x: lax.dynamic_index_in_dim(x, me_core, 2, keepdims=False)
    theirs = lambda x: lax.dynamic_index_in_dim(x, 1 - me_core, 2, keepdims=False)
    features = mine(features) + sibling(theirs(features))
    features = by_group(features.reshape(6, chips, groups, cut), 2)
    grad_bias_kv = col(grad_kv).reshape(2, channels) + jnp.stack([col(grad_halo), jnp.zeros((channels,), F32)])
    per_channel = jnp.concatenate(
        [ddecay, dfreq, dreal, dimag, dtaps, dstep, dskip, col(grad_query)[None], grad_bias_kv]
    )
    n_chan = per_channel.shape[0]
    tail = jnp.concatenate(
        [
            per_channel.reshape(n_chan, groups, chips, cut).transpose(1, 2, 0, 3).reshape(groups, chips, -1),
            features.transpose(2, 1, 0, 3).reshape(groups, chips, -1),
            grad_units_bias.reshape(groups, chips, -1),
        ],
        axis=-1,
    )
    used = tail.shape[-1]
    tail_rows = -(-used // (8 * width)) * 8
    tail = jnp.pad(tail, [(0, 0), (0, 0), (0, tail_rows * width - used)])
    tail = tail.reshape(groups, chips, tail_rows, width).astype(BF16)
    in_shares = lambda x: x.astype(BF16).reshape(groups, chips, cut, width)
    qo = fold_groups(in_shares(grad_wq), in_shares(grad_wo))
    kv = fold_groups(jnp.concatenate([in_shares(grad_wk), tail], axis=2), in_shares(grad_wv))
    mats = [*qo, *kv]
    sums = fold_z(jnp.concatenate(mats, axis=1)).astype(BF16)
    sums = spread(sums, "group", groups).astype(F32)
    wide = cut + tail_rows
    mat = lambda i, r=0: sums[:, i * cut + r : (i + 1) * cut + r].reshape(shard, width)
    tail = sums[:, 3 * cut : 2 * cut + wide].reshape(groups, -1)[:, :used]
    chan_part = tail[:, : n_chan * cut].reshape(groups, n_chan, cut).transpose(0, 2, 1).reshape(shard, n_chan)
    feat_part = tail[:, n_chan * cut : (n_chan + 6) * cut].reshape(groups, 6, cut).transpose(1, 0, 2).reshape(6, shard)
    sum_bias_up = tail[:, (n_chan + 6) * cut :].reshape(shard_units)
    modes = [chan_part[:, i * MODES : (i + 1) * MODES] for i in range(4)]
    sum_taps = chan_part[:, 4 * MODES : 4 * MODES + TAPS]
    singles = chan_part[:, 4 * MODES + TAPS :]
    return (
        output,
        grad_input,
        feat_part[0],
        feat_part[1],
        mat(0).T,
        singles[:, 2],
        mat(2).T,
        singles[:, 3],
        mat(3, tail_rows).T,
        singles[:, 4],
        sum_taps,
        singles[:, 0],
        modes[0],
        modes[1],
        modes[2],
        modes[3],
        singles[:, 1],
        mat(1),
        feat_part[2],
        feat_part[3],
        feat_part[4],
        ff[0].T,
        sum_bias_up,
        ff[1],
        feat_part[5],
    )


def solution(mesh):
    rows = P(("group", "chan"), None)
    columns, channels, vector, copied = P(None, "chan"), P("chan", None), P("chan"), P()
    return jax.shard_map(
        functools.partial(local, mesh.shape["group"], mesh.shape["chan"] // 2),
        mesh=mesh,
        in_specs=(
            rows, copied, copied, columns, vector, columns, vector, columns, vector, channels,
            vector, channels, channels, channels, channels, vector, channels, copied, copied, copied,
            columns, vector, channels, copied, rows, P("group", None),
        ),
        out_specs=(
            rows, rows, vector, vector, columns, vector, columns, vector, columns, vector,
            channels, vector, channels, channels, channels, channels, vector, channels, vector, vector,
            vector, columns, vector, channels, vector,
        ),
        check_vma=False,
    )
```

time: 1030 us -> 427 us (0.41); the launches traced: 1010 us -> 422 us
  local copies, waits for them, and re-layouts: 299 us -> 72.5 us
  waiting for transfers between devices: 286 us -> 109 us
  other arithmetic: 208 us -> 42.1 us
  matrix products: 143 us -> 21.7 us
  Pallas kernels: 0 us -> 82.9 us
  starting transfers between devices: 10.2 us -> 90 us
  blocking collectives: 44.4 us -> 0 us
  between operations: 18.6 us -> 4.48 us
    reduce_scatter x4 -> x0, waiting for transfers between devices: 201 us -> none  [the longest x1 71.9 us: channel_plan(): lax.psum_scatter(jnp.dot(core_low, w_out, preferred_element_type=jnp.floa...]
    dot_general x27 -> x14, matrix products: 143 us -> 21.7 us  [the longest x7 11.3 us: dot_nn(): lax.dot_general(a, b, (((1,), (0,)), ((), ())), preferred_element_type=F32)]
    pad x52 -> x1, local copies, waits for them, and re-layouts: 120 us -> 0.06 us  [local(): tail = jnp.pad(tail, [(0, 0), (0, 0), (0, tail_rows * width - used)])]
    scatter-add x1 -> x0, other arithmetic: 98.6 us -> none  [mixer_core(): toeplitz = jnp.where(lags >= 0, kernel[:, jnp.maximum(lags, 0)], 0.0)]
    all_gather x4 -> x0, waiting for transfers between devices: 84.5 us -> none  [the longest x1 33.8 us: channel_plan(): gathered_two = lax.all_gather(normed_two_low, 'chan', axis=0, tiled=True)]
    pallas_call x0 -> x5, Pallas kernels: none -> 82.9 us  [the longest x1 27.8 us: feed_forward(): pl.pallas_call(functools.partial(feed_forward_kernel, len(ups), up_at, do...]
    gather x2 -> x0, local copies, waits for them, and re-layouts: 63.2 us -> none  [mixer_core(): toeplitz = jnp.where(lags >= 0, kernel[:, jnp.maximum(lags, 0)], 0.0)]
    ppermute x0 -> x47, waiting for transfers between devices: none -> 55.2 us  [the longest x30 53.2 us: group_swap(): return lax.ppermute(x, 'group', [(i, i ^ bit) for i in range(groups)])]
  transfers between devices with their start and end apart: 9 -> 56, of which waited for: 6 -> 19; matrix products, arithmetic and copies ran while one was open for 32% -> 24% of each run, Pallas kernels for 0% -> 13%
where the time goes in v1:
time: 427 us; the launch traced here: 422 us
  waiting for transfers between devices  109 us (26%)
  starting transfers between devices  90 us (21%)
  Pallas kernels  82.9 us (19%)
  local copies, waits for them, and re-layouts  72.5 us (17%)
  other arithmetic  42.1 us (10%)
  matrix products  21.7 us (5%)
  between operations  4.48 us (1%)
    all_to_all x9, waiting for transfers between devices, swap(): return lax.all_to_all(x, axis, 0, 0, axis_index_groups=members, tiled=True)  53.6 us
    ppermute x30, waiting for transfers between devices, group_swap(): return lax.ppermute(x, 'group', [(i, i ^ bit) for i in range(groups)])  53.2 us
    all_to_all x9, starting transfers between devices, swap(): return lax.all_to_all(x, axis, 0, 0, axis_index_groups=members, tiled=True)  37.2 us
    ppermute x30, starting transfers between devices, group_swap(): return lax.ppermute(x, 'group', [(i, i ^ bit) for i in range(groups)])  33 us
    pallas_call x1, Pallas kernels, feed_forward(): pl.pallas_call(functools.partial(feed_forward_kernel, len(ups), up_at, do...  27.8 us
    unnamed x284, local copies, waits for them, and re-layouts  27.5 us
    pallas_call x1, Pallas kernels, grads(): self.call('ssm_grads', functools.partial(grads_kernel, self.steps, len(re...  17.7 us
    convert_element_type x12, other arithmetic, add(): return sum((x.astype(F32) for x in xs)).astype(BF16)  14.4 us
  transfers between devices with their start and end apart: 56, of which 19 were waited for; matrix products, arithmetic and copies ran while one was open for 24% of the time, Pallas kernels for 13%

profile of v1, /device:TPU:0, one launch (start us, length us, event | category | flops | bytes accessed | tf_op | source)
XLA Modules:
  0.0 422.5 jit_solution(17237111764903303768)
XLA Ops:
  1.6 4.3 %concatenate.93 = f32[141,96]{1,0:T(8,128)S(1)} concatenate(f32[32,96]{1,0:T(8,128)} %bitcast.302, f32[32,96]{1,0:T(8,128)} %bitcast.303, f32[32,96]{1,0:T(8,128)} %bitcast.304, f32[32,96]{1,0:T(8,128)} %bitcast.305, f32[4,96]{1,0:T(4,128)} %bitcast.311, f32[1,96]{1,0:T(1,128)} %bitcast.312, f32[1,96]{1,0:T(1,128)} %bitcast.313, f32[1,96]{1,0:T(1,128)} %bitcast.314, ...), dimensions={0} | concatenate | bytes 108288 | tf_op jit(solution)/shard_map/concatenate | solution.py:668
  6.6 6.3 %all-to-all-start.1 = ((f32[4,141,96]{2,1,0:T(8,128)}), f32[4,141,96]{2,1,0:T(8,128)S(1)}, u32[]{:S(2)}, u32[]{:S(2)}) async-start(f32[4,141,96]{2,1,0:T(8,128)} %broadcast_in_dim.39), calls=%async_computation.1 | async-start | bytes 589824 | tf_op jit(solution)/shard_map/all_to_all | solution.py:604
  23.6 2.3 collective-permute-start.1
  26.6 4.1 all-to-all-start
  37.4 3.5 all-to-all-done
  41.6 3.5 all-to-all-start.2
  46.8 1.6 collective-permute-start.2
  48.4 1.5 collective-permute-start.3
  49.9 3.3 all-to-all-done.2
  54.1 3.5 all-to-all-start.3
  58.3 1.5 collective-permute-start.9
  59.8 1.5 collective-permute-start.8
  62.4 1.5 collective-permute-start.4
  65.8 3.1 collective-permute-done.5
  68.9 1.5 collective-permute-start.14
  72.3 1.6 collective-permute-start.15
  73.9 1.5 collective-permute-start.10
  76.9 2.1 convolution_add_fusion.key.halo.value.refs_9_.refs_11_
  79.0 12.2 %ssm_before.1 = (f32[512,384]{1,0:T(8,128)S(1)}, f32[512,384]{1,0:T(8,128)S(1)}, f32[512,384]{1,0:T(8,128)S(1)}, f32[512,384]{1,0:T(8,128)S(1)}, f32[512,384]{1,...) custom-call(f32[2,2]{1,0:T(2,128)S(1)} %or_select_fusion.keeps, ...), custom_call_target="tpu_custom_call" | custom-call | flops 10000000000 | bytes 25000000 | tf_op jit(solution)/shard_map/ssm_before/pallas_call | solution.py:426
  94.8 3.9 collective-permute-start.11
  98.7 4.3 %collective-permute-start.12 = (bf16[64,384]{1,0:T(8,128)(2,1)S(1)}, bf16[64,384]{1,0:T(8,128)(2,1)S(1)}, u32[]{:S(2)}, u32[]{:S(2)}) collective-permute-start(bf16[64,384]{1,0:T(8,128)(2,1)S(1)} %get-tuple-element.81), channel_id=1, source_target_pairs={{0,4},{1,5},{2,6},{3,7},{8,12},{9,13},{10,14},{11,15},{16,20},{17,... | collective-permute-start | bytes 147464 | tf_op jit(solution)/shard_map/ppermute | solution.py:623
  105.0 2.0 broadcast_in_dim.44
  107.1 4.2 all-to-all-start.4
  111.3 12.7 %ssm_conv.1 = (f32[512,384]{1,0:T(8,128)S(1)}, bf16[512,384]{1,0:T(8,128)(2,1)S(1)}, f32[512,384]{1,0:T(8,128)S(1)}, f32[512,384]{1,0:T(8,128)S(1)}) custom-call(f32[2,2]{1,0:T(2,128)S(1)} %or_select_fusion.keeps, f32[2,4]{1,0:T(2,128)S(1)} %select_reduce_fusion.masks, f32[512,384]{1,0:T(8,128)S(1)} %get-tuple-element.77.x, ...), custom_call_target="tpu_custom_call" | custom-call | flops 10000000000 | bytes 25000000 | tf_op jit(solution)/shard_map/ssm_conv/pallas_call | solution.py:441
  124.1 3.0 fusion.54
  132.1 11.0 %collective-permute-done.21 = bf16[4,96,768]{2,1,0:T(8,128)(2,1)S(1)} collective-permute-done((bf16[4,96,768]{2,1,0:T(8,128)(2,1)S(1)}, bf16[4,96,768]{2,1,0:T(8,128)(2,1)S(1)}, u32[]{:S(2)}, u32[]{:S(2)}) %collective-permute-start.21) | collective-permute-done | bytes 589856 | tf_op jit(solution)/shard_map/ppermute | solution.py:616
  145.9 1.5 collective-permute-start.25
  147.4 1.8 fusion.121
  152.1 4.9 %collective-permute-done.20 = bf16[4,96,768]{2,1,0:T(8,128)(2,1)S(1)} collective-permute-done((bf16[4,96,768]{2,1,0:T(8,128)(2,1)S(1)}, bf16[4,96,768]{2,1,0:T(8,128)(2,1)S(1)}, u32[]{:S(2)}, u32[]{:S(2)}) %collective-permute-start.20) | collective-permute-done | bytes 589856 | tf_op jit(solution)/shard_map/ppermute | solution.py:616
  157.8 1.8 collective-permute-done.24
  160.3 8.6 %collective-permute-done.22 = bf16[4,96,768]{2,1,0:T(8,128)(2,1)} collective-permute-done((bf16[4,96,768]{2,1,0:T(8,128)(2,1)S(1)}, bf16[4,96,768]{2,1,0:T(8,128)(2,1)}, u32[]{:S(2)}, u32[]{:S(2)}) %collective-permute-start.22) | collective-permute-done | bytes 589856 | tf_op jit(solution)/shard_map/ppermute | solution.py:616
  168.9 2.0 collective-permute-done.25
  176.1 27.8 %feed_forward.1 = (f32[256,768]{1,0:T(8,128)}, f32[256,768]{1,0:T(8,128)}, f32[256,768]{1,0:T(8,128)}, f32[256,768]{1,0:T(8,128)}, f32[4,384]{1,0:T(4,128)S(1)},...) custom-call(bf16[256,768]{1,0:T(8,128)(2,1)S(1)} %copy-done.3, ...), custom_call_target="tpu_custom_call" | custom-call | flops 7247757312 | bytes 14155776 | tf_op jit(solution)/shard_map/feed_forward/pallas_call | solution.py:545
  204.4 2.0 collective-permute-done.27
  206.5 1.7 multiply_reduce_fusion.1
  208.2 1.6 fusion.102
  209.8 1.9 convert_element_type.248
  212.1 1.5 collective-permute-start.43
  217.6 1.6 fusion.24.grad_core
  219.3 12.4 %ssm_after.1 = (f32[512,384]{1,0:T(8,128)S(1)}, bf16[512,384]{1,0:T(8,128)(2,1)S(1)}, f32[512,384]{1,0:T(8,128)S(1)}, f32[512,384]{1,0:T(8,128)S(1)}, f32[512,38...) custom-call(f32[2,2]{1,0:T(2,128)S(1)} %copy-done.11, ...), custom_call_target="tpu_custom_call" | custom-call | flops 10000000000 | bytes 25000000 | tf_op jit(solution)/shard_map/ssm_after/pallas_call | solution.py:455
  235.8 5.0 %collective-permute-done.43 = bf16[2,384,768]{2,1,0:T(8,128)(2,1)} collective-permute-done((bf16[2,384,768]{2,1,0:T(8,128)(2,1)}, bf16[2,384,768]{2,1,0:T(8,128)(2,1)}, u32[]{:S(2)}, u32[]{:S(2)}) %collective-permute-start.43) | collective-permute-done | bytes 1179680 | tf_op jit(solution)/shard_map/ppermute | solution.py:616
  240.7 2.0 fusion.14
  247.6 2.1 fusion.15
  263.9 17.7 %ssm_grads.1 = (bf16[512,768]{1,0:T(8,128)(2,1)S(1)}, f32[8,384]{1,0:T(8,128)S(1)}, f32[32,384]{1,0:T(8,128)S(1)}, f32[32,384]{1,0:T(8,128)S(1)}, f32[32,384]{1,...) custom-call(f32[2,2]{1,0:T(2,128)S(1)} %copy-done.11, f32[2,4]{1,0:T(2,128)S(1)} %copy-done.9, ...), custom_call_target="tpu_custom_call" | custom-call | flops 15000000512 | bytes 37500000 | tf_op jit(solution)/shard_map/ssm_grads/pallas_call | solution.py:470
  283.1 2.6 fusion.122
  288.5 2.4 fusion.4
  290.9 1.8 fusion.106
  299.3 1.6 fusion.42
  302.3 1.6 fusion.39
  305.5 2.2 fusion.3
  307.7 1.6 collective-permute-start.37
  311.3 1.9 collective-permute-start.38
  315.8 1.5 collective-permute-start.39
  319.5 9.1 %collective-permute-done.39 = bf16[2,4,32,768]{3,2,1,0:T(8,128)(2,1)S(1)} collective-permute-done((bf16[2,4,32,768]{3,2,1,0:T(8,128)(2,1)S(1)}, bf16[2,4,32,768]{3,2,1,0:T(8,128)(2,1)S(1)}, u32[]{:S(2)}, u32[]{:S(2)}) %collective-permute-start.39) | collective-permute-done | bytes 393248 | tf_op jit(solution)/shard_map/ppermute | solution.py:616
  330.2 4.6 %collective-permute-done.40 = bf16[4,32,768]{2,1,0:T(8,128)(2,1)S(1)} collective-permute-done((bf16[4,32,768]{2,1,0:T(8,128)(2,1)S(1)}, bf16[4,32,768]{2,1,0:T(8,128)(2,1)S(1)}, u32[]{:S(2)}, u32[]{:S(2)}) %collective-permute-start.40) | collective-permute-done | bytes 196640 | tf_op jit(solution)/shard_map/ppermute | solution.py:616
  335.8 4.4 %all-to-all-start.5 = ((bf16[4,104,768]{2,1,0:T(8,128)(2,1)}), bf16[4,104,768]{2,1,0:T(8,128)(2,1)S(1)}, u32[]{:S(2)}, u32[]{:S(2)}) async-start(bf16[4,104,768]{2,1,0:T(8,128)(2,1)} %pad_maximum_fusion.4), calls=%async_computation.5 | async-start | bytes 1277952 | tf_op jit(solution)/shard_map/all_to_all | solution.py:604
  344.2 11.4 %all-to-all-done.5 = bf16[4,104,768]{2,1,0:T(8,128)(2,1)S(1)} async-done(((bf16[4,104,768]{2,1,0:T(8,128)(2,1)}), bf16[4,104,768]{2,1,0:T(8,128)(2,1)S(1)}, u32[]{:S(2)}, u32[]{:S(2)}) %all-to-all-start.5) | async-done | bytes 639008 | tf_op jit(solution)/shard_map/all_to_all | solution.py:604
  355.7 4.3 %all-to-all-start.7 = ((bf16[4,2,96,768]{3,2,1,0:T(8,128)(2,1)}), bf16[4,2,96,768]{3,2,1,0:T(8,128)(2,1)}, u32[]{:S(2)}, u32[]{:S(2)}) async-start(bf16[4,2,96,768]{3,2,1,0:T(8,128)(2,1)} %pad_maximum_fusion), calls=%async_computation.7 | async-start | bytes 2359296 | tf_op jit(solution)/shard_map/all_to_all | solution.py:604
  361.0 26.9 %all-to-all-done.7 = bf16[4,2,96,768]{3,2,1,0:T(8,128)(2,1)} async-done(((bf16[4,2,96,768]{3,2,1,0:T(8,128)(2,1)}), bf16[4,2,96,768]{3,2,1,0:T(8,128)(2,1)}, u32[]{:S(2)}, u32[]{:S(2)}) %all-to-all-start.7) | async-done | bytes 1179680 | tf_op jit(solution)/shard_map/all_to_all | solution.py:604
  388.8 3.5 all-to-all-start.6
  394.5 1.5 reduce_sum.215
  396.0 5.0 %all-to-all-done.6 = bf16[4,104,768]{2,1,0:T(8,128)(2,1)S(1)} async-done(((bf16[4,104,768]{2,1,0:T(8,128)(2,1)}), bf16[4,104,768]{2,1,0:T(8,128)(2,1)S(1)}, u32[]{:S(2)}, u32[]{:S(2)}) %all-to-all-start.6) | async-done | bytes 639008 | tf_op jit(solution)/shard_map/all_to_all | solution.py:604
  402.1 3.5 all-to-all-start.8
  416.0 3.5 all-to-all-done.8
  (532 shorter events, 123.8 us)
Async XLA Ops:
  6.6 19.2 %all-to-all-start.1 = ((f32[4,141,96]{2,1,0:T(8,128)}), f32[4,141,96]{2,1,0:T(8,128)S(1)}, u32[]{:S(2)}, u32[]{:S(2)}) async-start(f32[4,141,96]{2,1,0:T(8,128)} %broadcast_in_dim.39), calls=%async_computation.1 | async-start | bytes 589824 | tf_op jit(solution)/shard_map/all_to_all | solution.py:604
  13.6 8.3 %collective-permute-start = (bf16[8,768]{1,0:T(8,128)(2,1)S(1)}, bf16[8,768]{1,0:T(8,128)(2,1)S(1)}, u32[]{:S(2)}, u32[]{:S(2)}) collective-permute-start(bf16[8,768]{1,0:T(8,128)(2,1)S(1)} %slice.447), channel_id=1, source_target_pairs={{1,3},{3,5},{5,7},{9,11},{11,13},{13,15},{17,19},{19,21},{21,23},{... | collective-permute-start | bytes 36872 | tf_op jit(solution)/shard_map/ppermute | solution.py:711
  20.9 90.3 %copy-start.8 = (f32[2,4]{1,0:T(2,128)}, f32[2,4]{1,0:T(2,128)S(1)}, u32[]{:S(2)}) copy-start(f32[2,4]{1,0:T(2,128)S(1)} %select_reduce_fusion.masks) | copy-start | bytes 100
  21.6 89.7 %copy-start.10 = (f32[2,2]{1,0:T(2,128)}, f32[2,2]{1,0:T(2,128)S(1)}, u32[]{:S(2)}) copy-start(f32[2,2]{1,0:T(2,128)S(1)} %or_select_fusion.keeps) | copy-start | bytes 52
  23.6 12.7 %collective-permute-start.1 = (bf16[264,768]{1,0:T(8,128)(2,1)S(1)}, bf16[264,768]{1,0:T(8,128)(2,1)}, u32[]{:S(2)}, u32[]{:S(2)}) collective-permute-start(bf16[264,768]{1,0:T(8,128)(2,1)S(1)} %get-tuple-element.381), channel_id=1, source_target_pairs={{0,1},{1,0},{2,3},{3,2},{4,5},{5,4},{6,7},{7,6},{8,9},{9,8},{10,11... | collective-permute-start | bytes 1216520 | tf_op jit(solution)/shard_map/ppermute | solution.py:619
  26.6 14.2 %all-to-all-start = ((bf16[4,2,24,768]{3,2,1,0:T(8,128)(2,1)}), bf16[4,2,24,768]{3,2,1,0:T(8,128)(2,1)}, u32[]{:S(2)}, u32[]{:S(2)}) async-start(bf16[4,2,24,768]{3,2,1,0:T(8,128)(2,1)} %broadcast_in_dim.38), calls=%async_computation | async-start | bytes 589824 | tf_op jit(solution)/shard_map/all_to_all | solution.py:604
  35.9 75.3 %copy-start.6 = (f32[1,384]{1,0:T(1,128)}, f32[1,384]{1,0:T(1,128)S(1)}, u32[]{:S(2)}) copy-start(f32[1,384]{1,0:T(1,128)S(1)} %slice.478.refs_7_) | copy-start | bytes 4612
  37.4 39.5 %copy-start.58 = (bf16[256,768]{1,0:T(8,128)(2,1)}, bf16[256,768]{1,0:T(8,128)(2,1)S(1)}, u32[]{:S(2)}) copy-start(bf16[256,768]{1,0:T(8,128)(2,1)S(1)} %get-tuple-element.361) | copy-start | bytes 1179652
  37.4 39.5 %copy-start.62 = (bf16[256,768]{1,0:T(8,128)(2,1)}, bf16[256,768]{1,0:T(8,128)(2,1)S(1)}, u32[]{:S(2)}) copy-start(bf16[256,768]{1,0:T(8,128)(2,1)S(1)} %get-tuple-element.362) | copy-start | bytes 1179652
  41.6 11.6 %all-to-all-start.2 = ((bf16[4,2,24,768]{3,2,1,0:T(8,128)(2,1)}), bf16[4,2,24,768]{3,2,1,0:T(8,128)(2,1)S(1)}, u32[]{:S(2)}, u32[]{:S(2)}) async-start(bf16[4,2,24,768]{3,2,1,0:T(8,128)(2,1)} %broadcast_in_dim.40), calls=%async_computation.2 | async-start | bytes 589824 | tf_op jit(solution)/shard_map/all_to_all | solution.py:604
  46.8 15.0 %collective-permute-start.2 = (bf16[4,24,768]{2,1,0:T(8,128)(2,1)S(1)}, bf16[4,24,768]{2,1,0:T(8,128)(2,1)}, u32[]{:S(2)}, u32[]{:S(2)}) collective-permute-start(bf16[4,24,768]{2,1,0:T(8,128)(2,1)S(1)} %get-tuple-element.395), channel_id=1, source_target_pairs={{0,8},{8,0},{16,24},{24,16},{1,9},{9,1},{17,25},{25,17},{2,10},{10... | collective-permute-start | bytes 442376 | tf_op jit(solution)/shard_map/ppermute | solution.py:616
  48.4 14.1 %collective-permute-start.3 = (bf16[4,24,768]{2,1,0:T(8,128)(2,1)S(1)}, bf16[4,24,768]{2,1,0:T(8,128)(2,1)}, u32[]{:S(2)}, u32[]{:S(2)}) collective-permute-start(bf16[4,24,768]{2,1,0:T(8,128)(2,1)S(1)} %get-tuple-element.395), channel_id=1, source_target_pairs={{0,16},{8,24},{16,0},{24,8},{1,17},{9,25},{17,1},{25,9},{2,18},{10... | collective-permute-start | bytes 442376 | tf_op jit(solution)/shard_map/ppermute | solution.py:616
  54.1 51.0 %all-to-all-start.3 = ((bf16[4,96,768]{2,1,0:T(8,128)(2,1)}), bf16[4,96,768]{2,1,0:T(8,128)(2,1)S(1)}, u32[]{:S(2)}, u32[]{:S(2)}) async-start(bf16[4,96,768]{2,1,0:T(8,128)(2,1)} %broadcast_in_dim.42), calls=%async_computation.3 | async-start | bytes 1179648 | tf_op jit(solution)/shard_map/all_to_all | solution.py:604
  58.3 46.0 %copy-start.95 = (bf16[4,1,24,768]{3,2,1,0:T(8,128)(2,1)}, bf16[4,1,24,768]{3,2,1,0:T(8,128)(2,1)S(1)}, u32[]{:S(2)}) copy-start(bf16[4,1,24,768]{3,2,1,0:T(8,128)(2,1)S(1)} %get-tuple-element.393) | copy-start | bytes 442372
  58.3 14.0 %collective-permute-start.9 = (bf16[4,24,768]{2,1,0:T(8,128)(2,1)S(1)}, bf16[4,24,768]{2,1,0:T(8,128)(2,1)S(1)}, u32[]{:S(2)}, u32[]{:S(2)}) collective-permute-start(bf16[4,24,768]{2,1,0:T(8,128)(2,1)S(1)} %get-tuple-element.391), channel_id=1, source_target_pairs={{0,16},{8,24},{16,0},{24,8},{1,17},{9,25},{17,1},{25,9},{2,18},{10... | collective-permute-start | bytes 442376 | tf_op jit(solution)/shard_map/ppermute | solution.py:616
  59.8 38.9 %collective-permute-start.8 = (bf16[4,24,768]{2,1,0:T(8,128)(2,1)S(1)}, bf16[4,24,768]{2,1,0:T(8,128)(2,1)S(1)}, u32[]{:S(2)}, u32[]{:S(2)}) collective-permute-start(bf16[4,24,768]{2,1,0:T(8,128)(2,1)S(1)} %get-tuple-element.391), channel_id=1, source_target_pairs={{0,8},{8,0},{16,24},{24,16},{1,9},{9,1},{17,25},{25,17},{2,10},{10... | collective-permute-start | bytes 442376 | tf_op jit(solution)/shard_map/ppermute | solution.py:616
  61.3 7.6 %collective-permute-start.5 = (bf16[4,24,768]{2,1,0:T(8,128)(2,1)S(1)}, bf16[4,24,768]{2,1,0:T(8,128)(2,1)S(1)}, u32[]{:S(2)}, u32[]{:S(2)}) collective-permute-start(bf16[4,24,768]{2,1,0:T(8,128)(2,1)S(1)} %get-tuple-element.394), channel_id=1, source_target_pairs={{0,8},{8,0},{16,24},{24,16},{1,9},{9,1},{17,25},{25,17},{2,10},{10... | collective-permute-start | bytes 442376 | tf_op jit(solution)/shard_map/ppermute | solution.py:616
  61.9 12.0 %collective-permute-start.6 = (bf16[4,24,768]{2,1,0:T(8,128)(2,1)S(1)}, bf16[4,24,768]{2,1,0:T(8,128)(2,1)S(1)}, u32[]{:S(2)}, u32[]{:S(2)}) collective-permute-start(bf16[4,24,768]{2,1,0:T(8,128)(2,1)S(1)} %get-tuple-element.394), channel_id=1, source_target_pairs={{0,16},{8,24},{16,0},{24,8},{1,17},{9,25},{17,1},{25,9},{2,18},{10... | collective-permute-start | bytes 442376 | tf_op jit(solution)/shard_map/ppermute | solution.py:616
  62.4 9.3 %collective-permute-start.4 = (bf16[4,24,768]{2,1,0:T(8,128)(2,1)}, bf16[4,24,768]{2,1,0:T(8,128)(2,1)S(1)}, u32[]{:S(2)}, u32[]{:S(2)}) collective-permute-start(bf16[4,24,768]{2,1,0:T(8,128)(2,1)} %collective-permute-done.3), channel_id=1, source_target_pairs={{0,8},{8,0},{16,24},{24,16},{1,9},{9,1},{17,25},{25,17},{2,10},{10... | collective-permute-start | bytes 442376 | tf_op jit(solution)/shard_map/ppermute | solution.py:616
  68.9 6.5 %collective-permute-start.14 = (bf16[4,24,768]{2,1,0:T(8,128)(2,1)}, bf16[4,24,768]{2,1,0:T(8,128)(2,1)}, u32[]{:S(2)}, u32[]{:S(2)}) collective-permute-start(bf16[4,24,768]{2,1,0:T(8,128)(2,1)} %get-tuple-element.392), channel_id=1, source_target_pairs={{0,8},{8,0},{16,24},{24,16},{1,9},{9,1},{17,25},{25,17},{2,10},{10... | collective-permute-start | bytes 442376 | tf_op jit(solution)/shard_map/ppermute | solution.py:616
  71.7 5.1 %collective-permute-start.7 = (bf16[4,24,768]{2,1,0:T(8,128)(2,1)S(1)}, bf16[4,24,768]{2,1,0:T(8,128)(2,1)S(1)}, u32[]{:S(2)}, u32[]{:S(2)}) collective-permute-start(bf16[4,24,768]{2,1,0:T(8,128)(2,1)S(1)} %collective-permute-done.5), channel_id=1, source_target_pairs={{0,16},{8,24},{16,0},{24,8},{1,17},{9,25},{17,1},{25,9},{2,18},{10... | collective-permute-start | bytes 442376 | tf_op jit(solution)/shard_map/ppermute | solution.py:616
  72.3 32.1 %copy-start.124 = (bf16[4,24,768]{2,1,0:T(8,128)(2,1)}, bf16[4,24,768]{2,1,0:T(8,128)(2,1)S(1)}, u32[]{:S(2)}) copy-start(bf16[4,24,768]{2,1,0:T(8,128)(2,1)S(1)} %collective-permute-done.9) | copy-start | bytes 442372
  72.3 51.8 %collective-permute-start.15 = (bf16[4,24,768]{2,1,0:T(8,128)(2,1)}, bf16[4,24,768]{2,1,0:T(8,128)(2,1)}, u32[]{:S(2)}, u32[]{:S(2)}) collective-permute-start(bf16[4,24,768]{2,1,0:T(8,128)(2,1)} %get-tuple-element.392), channel_id=1, source_target_pairs={{0,16},{8,24},{16,0},{24,8},{1,17},{9,25},{17,1},{25,9},{2,18},{10... | collective-permute-start | bytes 442376 | tf_op jit(solution)/shard_map/ppermute | solution.py:616
  73.9 29.1 %collective-permute-start.10 = (bf16[4,24,768]{2,1,0:T(8,128)(2,1)S(1)}, bf16[4,24,768]{2,1,0:T(8,128)(2,1)S(1)}, u32[]{:S(2)}, u32[]{:S(2)}) collective-permute-start(bf16[4,24,768]{2,1,0:T(8,128)(2,1)S(1)} %collective-permute-done.9), channel_id=1, source_target_pairs={{0,8},{8,0},{16,24},{24,16},{1,9},{9,1},{17,25},{25,17},{2,10},{10... | collective-permute-start | bytes 442376 | tf_op jit(solution)/shard_map/ppermute | solution.py:616
  75.4 48.7 %collective-permute-start.16 = (bf16[4,24,768]{2,1,0:T(8,128)(2,1)}, bf16[4,24,768]{2,1,0:T(8,128)(2,1)}, u32[]{:S(2)}, u32[]{:S(2)}) collective-permute-start(bf16[4,24,768]{2,1,0:T(8,128)(2,1)} %collective-permute-done.14), channel_id=1, source_target_pairs={{0,16},{8,24},{16,0},{24,8},{1,17},{9,25},{17,1},{25,9},{2,18},{10... | collective-permute-start | bytes 442376 | tf_op jit(solution)/shard_map/ppermute | solution.py:616
  94.8 16.4 %collective-permute-start.11 = (bf16[64,384]{1,0:T(8,128)(2,1)S(1)}, bf16[64,384]{1,0:T(8,128)(2,1)S(1)}, u32[]{:S(2)}, u32[]{:S(2)}) collective-permute-start(bf16[64,384]{1,0:T(8,128)(2,1)S(1)} %get-tuple-element.81), channel_id=1, source_target_pairs={{0,2},{1,3},{2,4},{3,5},{4,6},{5,7},{8,10},{9,11},{10,12},{11,13},... | collective-permute-start | bytes 147464 | tf_op jit(solution)/shard_map/ppermute | solution.py:623
  98.7 12.5 %collective-permute-start.12 = (bf16[64,384]{1,0:T(8,128)(2,1)S(1)}, bf16[64,384]{1,0:T(8,128)(2,1)S(1)}, u32[]{:S(2)}, u32[]{:S(2)}) collective-permute-start(bf16[64,384]{1,0:T(8,128)(2,1)S(1)} %get-tuple-element.81), channel_id=1, source_target_pairs={{0,4},{1,5},{2,6},{3,7},{8,12},{9,13},{10,14},{11,15},{16,20},{17,... | collective-permute-start | bytes 147464 | tf_op jit(solution)/shard_map/ppermute | solution.py:623
  103.0 8.2 %collective-permute-start.13 = (bf16[64,384]{1,0:T(8,128)(2,1)S(1)}, bf16[64,384]{1,0:T(8,128)(2,1)S(1)}, u32[]{:S(2)}, u32[]{:S(2)}) collective-permute-start(bf16[64,384]{1,0:T(8,128)(2,1)S(1)} %get-tuple-element.81), channel_id=1, source_target_pairs={{0,6},{1,7},{8,14},{9,15},{16,22},{17,23},{24,30},{25,31}} | collective-permute-start | bytes 147464 | tf_op jit(solution)/shard_map/ppermute | solution.py:623
  107.1 20.9 %all-to-all-start.4 = ((bf16[4,96,768]{2,1,0:T(8,128)(2,1)}), bf16[4,96,768]{2,1,0:T(8,128)(2,1)}, u32[]{:S(2)}, u32[]{:S(2)}) async-start(bf16[4,96,768]{2,1,0:T(8,128)(2,1)} %broadcast_in_dim.44), calls=%async_computation.4 | async-start | bytes 1179648 | tf_op jit(solution)/shard_map/all_to_all | solution.py:604
  127.2 18.7 %collective-permute-start.17 = (f32[256,768]{1,0:T(8,128)}, f32[256,768]{1,0:T(8,128)}, u32[]{:S(2)}, u32[]{:S(2)}) collective-permute-start(f32[256,768]{1,0:T(8,128)} %fusion.54), channel_id=1, source_target_pairs={{0,1},{1,0},{2,3},{3,2},{4,5},{5,4},{6,7},{7,6},{8,9},{9,8},{10,11... | collective-permute-start | bytes 2359304 | tf_op jit(solution)/shard_map/ppermute | solution.py:619
  127.3 15.7 %collective-permute-start.21 = (bf16[4,96,768]{2,1,0:T(8,128)(2,1)S(1)}, bf16[4,96,768]{2,1,0:T(8,128)(2,1)S(1)}, u32[]{:S(2)}, u32[]{:S(2)}) collective-permute-start(bf16[4,96,768]{2,1,0:T(8,128)(2,1)S(1)} %all-to-all-done.3), channel_id=1, source_target_pairs={{0,16},{8,24},{16,0},{24,8},{1,17},{9,25},{17,1},{25,9},{2,18},{10... | collective-permute-start | bytes 1769480 | tf_op jit(solution)/shard_map/ppermute | solution.py:616
  127.9 16.5 %collective-permute-start.23 = (bf16[4,96,768]{2,1,0:T(8,128)(2,1)}, bf16[4,96,768]{2,1,0:T(8,128)(2,1)}, u32[]{:S(2)}, u32[]{:S(2)}) collective-permute-start(bf16[4,96,768]{2,1,0:T(8,128)(2,1)} %all-to-all-done.4), channel_id=1, source_target_pairs={{0,8},{8,0},{16,24},{24,16},{1,9},{9,1},{17,25},{25,17},{2,10},{10... | collective-permute-start | bytes 1769480 | tf_op jit(solution)/shard_map/ppermute | solution.py:616
  129.6 20.1 %collective-permute-start.19 = (bf16[256,768]{1,0:T(8,128)(2,1)S(1)}, bf16[256,768]{1,0:T(8,128)(2,1)S(1)}, u32[]{:S(2)}, u32[]{:S(2)}) collective-permute-start(bf16[256,768]{1,0:T(8,128)(2,1)S(1)} %bitcast.227), channel_id=1, source_target_pairs={{0,1},{1,0},{2,3},{3,2},{4,5},{5,4},{6,7},{7,6},{8,9},{9,8},{10,11... | collective-permute-start | bytes 1179656 | tf_op jit(solution)/shard_map/ppermute | solution.py:619
  131.4 25.6 %collective-permute-start.20 = (bf16[4,96,768]{2,1,0:T(8,128)(2,1)S(1)}, bf16[4,96,768]{2,1,0:T(8,128)(2,1)S(1)}, u32[]{:S(2)}, u32[]{:S(2)}) collective-permute-start(bf16[4,96,768]{2,1,0:T(8,128)(2,1)S(1)} %all-to-all-done.3), channel_id=1, source_target_pairs={{0,8},{8,0},{16,24},{24,16},{1,9},{9,1},{17,25},{25,17},{2,10},{10... | collective-permute-start | bytes 1769480 | tf_op jit(solution)/shard_map/ppermute | solution.py:616
  143.0 16.5 %collective-permute-start.24 = (bf16[4,96,768]{2,1,0:T(8,128)(2,1)}, bf16[4,96,768]{2,1,0:T(8,128)(2,1)}, u32[]{:S(2)}, u32[]{:S(2)}) collective-permute-start(bf16[4,96,768]{2,1,0:T(8,128)(2,1)} %all-to-all-done.4), channel_id=1, source_target_pairs={{0,16},{8,24},{16,0},{24,8},{1,17},{9,25},{17,1},{25,9},{2,18},{10... | collective-permute-start | bytes 1769480 | tf_op jit(solution)/shard_map/ppermute | solution.py:616
  144.4 24.5 %collective-permute-start.22 = (bf16[4,96,768]{2,1,0:T(8,128)(2,1)S(1)}, bf16[4,96,768]{2,1,0:T(8,128)(2,1)}, u32[]{:S(2)}, u32[]{:S(2)}) collective-permute-start(bf16[4,96,768]{2,1,0:T(8,128)(2,1)S(1)} %collective-permute-done.21), channel_id=1, source_target_pairs={{0,8},{8,0},{16,24},{24,16},{1,9},{9,1},{17,25},{25,17},{2,10},{10... | collective-permute-start | bytes 1769480 | tf_op jit(solution)/shard_map/ppermute | solution.py:616
  145.9 25.1 %collective-permute-start.25 = (bf16[4,96,768]{2,1,0:T(8,128)(2,1)}, bf16[4,96,768]{2,1,0:T(8,128)(2,1)}, u32[]{:S(2)}, u32[]{:S(2)}) collective-permute-start(bf16[4,96,768]{2,1,0:T(8,128)(2,1)} %collective-permute-done.23), channel_id=1, source_target_pairs={{0,16},{8,24},{16,0},{24,8},{1,17},{9,25},{17,1},{25,9},{2,18},{10... | collective-permute-start | bytes 1769480 | tf_op jit(solution)/shard_map/ppermute | solution.py:616
  150.5 9.1 %collective-permute-start.18 = (bf16[256,768]{1,0:T(8,128)(2,1)S(1)}, bf16[256,768]{1,0:T(8,128)(2,1)S(1)}, u32[]{:S(2)}, u32[]{:S(2)}) collective-permute-start(bf16[256,768]{1,0:T(8,128)(2,1)S(1)} %add_convert_fusion.5.refs_0_), channel_id=1, source_target_pairs={{0,1},{1,0},{2,3},{3,2},{4,5},{5,4},{6,7},{7,6},{8,9},{9,8},{10,11... | collective-permute-start | bytes 1179656 | tf_op jit(solution)/shard_map/ppermute | solution.py:619
  203.9 2.5 collective-permute-start.27
  203.9 4.3 %collective-permute-start.26 = (f32[256,768]{1,0:T(8,128)}, f32[256,768]{1,0:T(8,128)S(1)}, u32[]{:S(2)}, u32[]{:S(2)}) collective-permute-start(f32[256,768]{1,0:T(8,128)} %get-tuple-element.84), channel_id=1, source_target_pairs={{0,1},{1,0},{2,3},{3,2},{4,5},{5,4},{6,7},{7,6},{8,9},{9,8},{10,11... | collective-permute-start | bytes 2359304 | tf_op jit(solution)/shard_map/ppermute | solution.py:619
  211.7 4.6 %collective-permute-start.28 = (bf16[256,768]{1,0:T(8,128)(2,1)}, bf16[256,768]{1,0:T(8,128)(2,1)}, u32[]{:S(2)}, u32[]{:S(2)}) collective-permute-start(bf16[256,768]{1,0:T(8,128)(2,1)} %convert_element_type.248), channel_id=1, source_target_pairs={{0,1},{1,0},{2,3},{3,2},{4,5},{5,4},{6,7},{7,6},{8,9},{9,8},{10,11... | collective-permute-start | bytes 1179656 | tf_op jit(solution)/shard_map/ppermute | solution.py:619
  212.1 28.6 %collective-permute-start.43 = (bf16[2,384,768]{2,1,0:T(8,128)(2,1)}, bf16[2,384,768]{2,1,0:T(8,128)(2,1)}, u32[]{:S(2)}, u32[]{:S(2)}) collective-permute-start(bf16[2,384,768]{2,1,0:T(8,128)(2,1)} %get-tuple-element.112), channel_id=1, source_target_pairs={{0,8},{8,0},{16,24},{24,16},{1,9},{9,1},{17,25},{25,17},{2,10},{10... | collective-permute-start | bytes 3538952 | tf_op jit(solution)/shard_map/ppermute | solution.py:616
  213.7 33.9 %collective-permute-start.45 = (bf16[2,384,768]{2,1,0:T(8,128)(2,1)}, bf16[2,384,768]{2,1,0:T(8,128)(2,1)}, u32[]{:S(2)}, u32[]{:S(2)}) collective-permute-start(bf16[2,384,768]{2,1,0:T(8,128)(2,1)} %get-tuple-element.115), channel_id=1, source_target_pairs={{0,16},{8,24},{16,0},{24,8},{1,17},{9,25},{17,1},{25,9},{2,18},{10... | collective-permute-start | bytes 3538952 | tf_op jit(solution)/shard_map/ppermute | solution.py:616
  231.7 23.3 %collective-permute-start.29 = (bf16[64,384]{1,0:T(8,128)(2,1)S(1)}, bf16[64,384]{1,0:T(8,128)(2,1)S(1)}, u32[]{:S(2)}, u32[]{:S(2)}) collective-permute-start(bf16[64,384]{1,0:T(8,128)(2,1)S(1)} %get-tuple-element.98), channel_id=1, source_target_pairs={{2,0},{3,1},{4,2},{5,3},{6,4},{7,5},{10,8},{11,9},{12,10},{13,11},... | collective-permute-start | bytes 147464 | tf_op jit(solution)/shard_map/ppermute | solution.py:623
  233.2 22.4 %collective-permute-start.30 = (bf16[64,384]{1,0:T(8,128)(2,1)S(1)}, bf16[64,384]{1,0:T(8,128)(2,1)S(1)}, u32[]{:S(2)}, u32[]{:S(2)}) collective-permute-start(bf16[64,384]{1,0:T(8,128)(2,1)S(1)} %get-tuple-element.98), channel_id=1, source_target_pairs={{4,0},{5,1},{6,2},{7,3},{12,8},{13,9},{14,10},{15,11},{20,16},{21,... | collective-permute-start | bytes 147464 | tf_op jit(solution)/shard_map/ppermute | solution.py:623
  234.5 22.6 %collective-permute-start.31 = (bf16[64,384]{1,0:T(8,128)(2,1)S(1)}, bf16[64,384]{1,0:T(8,128)(2,1)S(1)}, u32[]{:S(2)}, u32[]{:S(2)}) collective-permute-start(bf16[64,384]{1,0:T(8,128)(2,1)S(1)} %get-tuple-element.98), channel_id=1, source_target_pairs={{6,0},{7,1},{14,8},{15,9},{22,16},{23,17},{30,24},{31,25}} | collective-permute-start | bytes 147464 | tf_op jit(solution)/shard_map/ppermute | solution.py:623
  242.8 97.4 %collective-permute-start.44 = (bf16[384,768]{1,0:T(8,128)(2,1)}, bf16[384,768]{1,0:T(8,128)(2,1)}, u32[]{:S(2)}, u32[]{:S(2)}) collective-permute-start(bf16[384,768]{1,0:T(8,128)(2,1)} %fusion.14), channel_id=1, source_target_pairs={{0,16},{8,24},{16,0},{24,8},{1,17},{9,25},{17,1},{25,9},{2,18},{10... | collective-permute-start | bytes 1769480 | tf_op jit(solution)/shard_map/ppermute | solution.py:616
  249.7 92.0 %collective-permute-start.46 = (bf16[384,768]{1,0:T(8,128)(2,1)}, bf16[384,768]{1,0:T(8,128)(2,1)}, u32[]{:S(2)}, u32[]{:S(2)}) collective-permute-start(bf16[384,768]{1,0:T(8,128)(2,1)} %fusion.15), channel_id=1, source_target_pairs={{0,8},{8,0},{16,24},{24,16},{1,9},{9,1},{17,25},{25,17},{2,10},{10... | collective-permute-start | bytes 1769480 | tf_op jit(solution)/shard_map/ppermute | solution.py:616
  255.0 43.6 %collective-permute-start.34 = (bf16[2,4,24,768]{3,2,1,0:T(8,128)(2,1)}, bf16[2,4,24,768]{3,2,1,0:T(8,128)(2,1)}, u32[]{:S(2)}, u32[]{:S(2)}) collective-permute-start(bf16[2,4,24,768]{3,2,1,0:T(8,128)(2,1)} %pad_maximum_fusion.12), channel_id=1, source_target_pairs={{0,8},{8,0},{16,24},{24,16},{1,9},{9,1},{17,25},{25,17},{2,10},{10... | collective-permute-start | bytes 884744 | tf_op jit(solution)/shard_map/ppermute | solution.py:616
  255.6 45.3 %collective-permute-start.36 = (bf16[2,4,24,768]{3,2,1,0:T(8,128)(2,1)}, bf16[2,4,24,768]{3,2,1,0:T(8,128)(2,1)}, u32[]{:S(2)}, u32[]{:S(2)}) collective-permute-start(bf16[2,4,24,768]{3,2,1,0:T(8,128)(2,1)} %pad_maximum_fusion.13), channel_id=1, source_target_pairs={{0,16},{8,24},{16,0},{24,8},{1,17},{9,25},{17,1},{25,9},{2,18},{10... | collective-permute-start | bytes 884744 | tf_op jit(solution)/shard_map/ppermute | solution.py:616
  287.3 16.7 %collective-permute-start.32 = (f32[264,768]{1,0:T(8,128)}, f32[264,768]{1,0:T(8,128)}, u32[]{:S(2)}, u32[]{:S(2)}) collective-permute-start(f32[264,768]{1,0:T(8,128)} %pad_maximum_fusion.1), channel_id=1, source_target_pairs={{0,1},{1,0},{2,3},{3,2},{4,5},{5,4},{6,7},{7,6},{8,9},{9,8},{10,11... | collective-permute-start | bytes 2433032 | tf_op jit(solution)/shard_map/ppermute | solution.py:619
  298.6 12.7 %collective-permute-start.41 = (bf16[2,4,24,768]{3,2,1,0:T(8,128)(2,1)}, bf16[2,4,24,768]{3,2,1,0:T(8,128)(2,1)}, u32[]{:S(2)}, u32[]{:S(2)}) collective-permute-start(bf16[2,4,24,768]{3,2,1,0:T(8,128)(2,1)} %pad_maximum_fusion.14), channel_id=1, source_target_pairs={{0,16},{8,24},{16,0},{24,8},{1,17},{9,25},{17,1},{25,9},{2,18},{10... | collective-permute-start | bytes 884744 | tf_op jit(solution)/shard_map/ppermute | solution.py:616
  300.9 14.9 %collective-permute-start.35 = (bf16[4,24,768]{2,1,0:T(8,128)(2,1)}, bf16[4,24,768]{2,1,0:T(8,128)(2,1)}, u32[]{:S(2)}, u32[]{:S(2)}) collective-permute-start(bf16[4,24,768]{2,1,0:T(8,128)(2,1)} %fusion.42), channel_id=1, source_target_pairs={{0,16},{8,24},{16,0},{24,8},{1,17},{9,25},{17,1},{25,9},{2,18},{10... | collective-permute-start | bytes 442376 | tf_op jit(solution)/shard_map/ppermute | solution.py:616
  304.7 3.1 collective-permute-start.33
  307.7 10.7 %collective-permute-start.37 = (bf16[4,24,768]{2,1,0:T(8,128)(2,1)}, bf16[4,24,768]{2,1,0:T(8,128)(2,1)}, u32[]{:S(2)}, u32[]{:S(2)}) collective-permute-start(bf16[4,24,768]{2,1,0:T(8,128)(2,1)} %fusion.39), channel_id=1, source_target_pairs={{0,8},{8,0},{16,24},{24,16},{1,9},{9,1},{17,25},{25,17},{2,10},{10... | collective-permute-start | bytes 442376 | tf_op jit(solution)/shard_map/ppermute | solution.py:616
  311.3 2.9 collective-permute-start.38
  314.2 15.0 %collective-permute-start.42 = (bf16[4,24,768]{2,1,0:T(8,128)(2,1)S(1)}, bf16[4,24,768]{2,1,0:T(8,128)(2,1)S(1)}, u32[]{:S(2)}, u32[]{:S(2)}) collective-permute-start(bf16[4,24,768]{2,1,0:T(8,128)(2,1)S(1)} %fusion.36), channel_id=1, source_target_pairs={{0,8},{8,0},{16,24},{24,16},{1,9},{9,1},{17,25},{25,17},{2,10},{10... | collective-permute-start | bytes 442376 | tf_op jit(solution)/shard_map/ppermute | solution.py:616
  315.8 12.8 %collective-permute-start.39 = (bf16[2,4,32,768]{3,2,1,0:T(8,128)(2,1)S(1)}, bf16[2,4,32,768]{3,2,1,0:T(8,128)(2,1)S(1)}, u32[]{:S(2)}, u32[]{:S(2)}) collective-permute-start(bf16[2,4,32,768]{3,2,1,0:T(8,128)(2,1)S(1)} %pad_maximum_fusion.11), channel_id=1, source_target_pairs={{0,8},{8,0},{16,24},{24,16},{1,9},{9,1},{17,25},{25,17},{2,10},{10... | collective-permute-start | bytes 1179656 | tf_op jit(solution)/shard_map/ppermute | solution.py:616
  328.7 6.2 %collective-permute-start.40 = (bf16[4,32,768]{2,1,0:T(8,128)(2,1)S(1)}, bf16[4,32,768]{2,1,0:T(8,128)(2,1)S(1)}, u32[]{:S(2)}, u32[]{:S(2)}) collective-permute-start(bf16[4,32,768]{2,1,0:T(8,128)(2,1)S(1)} %fusion.46), channel_id=1, source_target_pairs={{0,16},{8,24},{16,0},{24,8},{1,17},{9,25},{17,1},{25,9},{2,18},{10... | collective-permute-start | bytes 589832 | tf_op jit(solution)/shard_map/ppermute | solution.py:616
  335.8 19.9 %all-to-all-start.5 = ((bf16[4,104,768]{2,1,0:T(8,128)(2,1)}), bf16[4,104,768]{2,1,0:T(8,128)(2,1)S(1)}, u32[]{:S(2)}, u32[]{:S(2)}) async-start(bf16[4,104,768]{2,1,0:T(8,128)(2,1)} %pad_maximum_fusion.4), calls=%async_computation.5 | async-start | bytes 1277952 | tf_op jit(solution)/shard_map/all_to_all | solution.py:604
  355.7 32.3 %all-to-all-start.7 = ((bf16[4,2,96,768]{3,2,1,0:T(8,128)(2,1)}), bf16[4,2,96,768]{3,2,1,0:T(8,128)(2,1)}, u32[]{:S(2)}, u32[]{:S(2)}) async-start(bf16[4,2,96,768]{3,2,1,0:T(8,128)(2,1)} %pad_maximum_fusion), calls=%async_computation.7 | async-start | bytes 2359296 | tf_op jit(solution)/shard_map/all_to_all | solution.py:604
  361.0 31.3 %copy-start.52 = (f32[264,768]{1,0:T(8,128)S(1)}, f32[264,768]{1,0:T(8,128)}, u32[]{:S(2)}) copy-start(f32[264,768]{1,0:T(8,128)} %get-tuple-element.380) | copy-start | bytes 2433028
  388.8 12.2 %all-to-all-start.6 = ((bf16[4,104,768]{2,1,0:T(8,128)(2,1)}), bf16[4,104,768]{2,1,0:T(8,128)(2,1)S(1)}, u32[]{:S(2)}, u32[]{:S(2)}) async-start(bf16[4,104,768]{2,1,0:T(8,128)(2,1)} %broadcast_in_dim.45), calls=%async_computation.6 | async-start | bytes 1277952 | tf_op jit(solution)/shard_map/all_to_all | solution.py:604
  402.1 17.4 %all-to-all-start.8 = ((bf16[4,2,96,768]{3,2,1,0:T(8,128)(2,1)}), bf16[4,2,96,768]{3,2,1,0:T(8,128)(2,1)S(1)}, u32[]{:S(2)}, u32[]{:S(2)}) async-start(bf16[4,2,96,768]{3,2,1,0:T(8,128)(2,1)} %broadcast_in_dim.46), calls=%async_computation.8 | async-start | bytes 2359296 | tf_op jit(solution)/shard_map/all_to_all | solution.py:604
  (124 other events, 866.5 us)
